TPU v7x, 256 devices: a whole 4x4x8 slice. The times are simulated.
256 devices in a mesh: gx: 8 (over z), gy: 4 (over x_lo, core), gz: 8 (over y, x_hi).
Axes of the slice: x: 4 (x_hi: 2, x_lo: 2; x = x_hi * 2 + x_lo), y: 4, z: 8, core: 2. Of those that a mesh axis runs over, the one named last changes fastest.
Arguments:
- recovery_temp: float32 [8192, 128], P(('gx', 'gy', 'gz')), may hold values from 2 to 4
- film_coeff: float32 [8192, 128], P(('gx', 'gy', 'gz')), may hold values from 0.5 to 4
- emissivity: float32 [8192, 128], P(('gx', 'gy', 'gz')), may hold values from 0.6 to 0.95
- char_density: float32 [8192, 128], P(('gx', 'gy', 'gz')), may hold values from 0.5 to 2
- back_temp: float32 [8192, 128], P(('gx', 'gy', 'gz')), may hold values from 0.8 to 1.2
- stencil_frac: float32 [8192, 128], P(('gx', 'gy', 'gz')), may hold values from 0 to 1
- wall_owner: int32 [8192, 1], P(('gx', 'gy', 'gz')), may hold values from 0 to 3; in each aligned block of 32 rows (0 to 31, 32 to 63, ...) at most 16 rows name the same one
- stencil_start: int32 [8192], P(('gx', 'gy', 'gz')), may hold values from 0 to 1023
- live_count: int32 [8192], P(('gx', 'gy', 'gz')), may hold values from 1 to 128
- wall_mask: int32 [256, 128], P('gx', 'gy'), may hold values 0 or 1
- wall_dir: float32 [3, 256, 128], P(None, 'gx', 'gy'), may hold values from -4 to 4
- stiffness: float32 [256, 128, 1024], P('gx', 'gy', 'gz'), may hold values from 0.2 to 5
- start_disp: float32 [3, 256, 128, 1024], P(None, 'gx', 'gy', 'gz'), may hold values from -6 to 6
Outputs:
- surface_temp: float32 [8192, 128], P(('gx', 'gy', 'gz'))
- displacement: float32 [3, 256, 128, 1024], P(None, 'gx', 'gy', 'gz')
Inputs may be any that keep to these rules, and one draw needn't show every extreme that they name: `wall_owner`: among the 32 tiles of one device, at most 16 name the same owner, a bound that some block reaches of them.
All inputs are finite; a program needn't handle non-finite values. No bound on the sum of `wall_mask` on one device may be relied on, other than what follows from the above.
Results may differ from a plain program's by a relative error of at most 0.00002.
Values sent between devices are 32-bit elements; how exact they have to be, the bound alone decides.
A program may use at most 256 MiB of HBM per device.

v0:
```python
import jax
import jax.numpy as jnp
from jax import lax
from jax.sharding import PartitionSpec as P

NEWTON = 6
SWEEPS = 4
CAP = 16


arrhenius_scale = 0.5
activation = 3.0
blowing = 0.5
heat_release = 0.3
radiation = 0.05
conduction = 0.5
time_step = 1.5


def extended(block, sides, width):
    for axis, dim in sides:
        count = lax.axis_size(axis)
        forward = [(i, i + 1) for i in range(count - 1)]
        backward = [(target, source) for source, target in forward]
        low = lax.ppermute(
            lax.slice_in_dim(block, block.shape[dim] - width, None, axis=dim), axis, forward
        )
        high = lax.ppermute(lax.slice_in_dim(block, 0, width, axis=dim), axis, backward)
        block = jnp.concatenate([low, block, high], axis=dim)
    return block


def ablation_rate(surface):
    return arrhenius_scale * jnp.exp(activation * (1.0 - 1.0 / surface))


def balance_step(surface, recovery_temp, film_coeff, emissivity, back_temp):
    ablate = ablation_rate(surface)
    factor = 1.0 / (1.0 + blowing * ablate / film_coeff)
    imbalance = (
        film_coeff * factor * (recovery_temp - surface)
        + heat_release * ablate
        - radiation * emissivity * surface**4
        - conduction * (surface - back_temp)
    )
    slope = film_coeff * factor + 4.0 * radiation * emissivity * surface**3 + conduction
    return surface + imbalance / slope


def node_terms(recession, stencil_frac, live_count):
    width = recession.shape[1]
    live = (jnp.arange(width, dtype=jnp.int32)[None, :] < live_count[:, None]).astype(jnp.float32)
    upper = stencil_frac * live
    lower = (1.0 - stencil_frac) * live
    return jnp.stack([lower * recession, upper * recession, lower, upper], axis=1)


def deposit(terms, starts, cells, segments):
    width = terms.shape[2]
    offsets = jnp.arange(width, dtype=jnp.int32)[None, :]
    first = ((starts[:, None] + offsets) % cells).reshape(-1)
    second = ((starts[:, None] + offsets + 1) % cells).reshape(-1)
    numer = jax.ops.segment_sum(
        terms[:, 0].reshape(-1), first, num_segments=segments
    ) + jax.ops.segment_sum(terms[:, 1].reshape(-1), second, num_segments=segments)
    denom = jax.ops.segment_sum(
        terms[:, 2].reshape(-1), first, num_segments=segments
    ) + jax.ops.segment_sum(terms[:, 3].reshape(-1), second, num_segments=segments)
    return (numer, denom)


def relax(padded, padded_k):
    center_k = padded_k[1:-1, 1:-1, 1:-1]
    inner = slice(1, -1)
    shifts = [
        (slice(2, None), inner, inner),
        (slice(None, -2), inner, inner),
        (inner, slice(2, None), inner),
        (inner, slice(None, -2), inner),
        (inner, inner, slice(2, None)),
        (inner, inner, slice(None, -2)),
    ]
    total = None
    weight = None
    for picked in shifts:
        spring = 0.5 * (center_k + padded_k[picked])
        value = padded[..., picked[0], picked[1], picked[2]]
        if total is None:
            total = spring * value
            weight = spring
        else:
            total = total + spring * value
            weight = weight + spring
    return total / weight


def local(
    recovery_temp,
    film_coeff,
    emissivity,
    char_density,
    back_temp,
    stencil_frac,
    wall_owner,
    stencil_start,
    live_count,
    wall_mask,
    wall_dir,
    stiffness,
    start_disp,
):
    surface = back_temp
    for iteration in range(NEWTON):
        surface = balance_step(surface, recovery_temp, film_coeff, emissivity, back_temp)
    recession = time_step * ablation_rate(surface) / char_density
    terms = node_terms(recession, stencil_frac, live_count)
    size_x, size_y, size_z = stiffness.shape
    cells = size_x * size_y
    owners = lax.axis_size("gy")
    owner_row = wall_owner[:, 0]
    onehot = (owner_row[:, None] == jnp.arange(owners, dtype=jnp.int32)[None, :]).astype(jnp.int32)
    slot = jnp.sum((jnp.cumsum(onehot, axis=0) - onehot) * onehot, axis=1)
    width = terms.shape[2]
    outgoing = jnp.zeros((owners, CAP, 4, width), jnp.float32).at[owner_row, slot].set(terms)
    out_starts = (
        jnp.zeros((owners, CAP), jnp.float32)
        .at[owner_row, slot]
        .set(stencil_start.astype(jnp.float32))
    )
    arrived, arrived_starts = (
        lax.all_to_all(outgoing, "gy", split_axis=0, concat_axis=0, tiled=True),
        lax.all_to_all(out_starts, "gy", split_axis=0, concat_axis=0, tiled=True),
    )
    arrived = arrived.reshape(owners * CAP, 4, width)
    arrived_starts = arrived_starts.reshape(-1).astype(jnp.int32)
    local_numer, local_denom = deposit(arrived, arrived_starts, cells, cells)
    summed = lax.psum(jnp.stack([local_numer, local_denom], axis=0), "gz")
    numer = summed[0]
    denom = summed[1]
    face = (numer / (1.0 + denom)).reshape(size_x, size_y)
    on_wall = (lax.axis_index("gz") == 0).astype(jnp.float32)
    ghost = -wall_mask.astype(jnp.float32) * face * wall_dir * on_wall
    padded_k = extended(stiffness, (("gx", 0), ("gy", 1), ("gz", 2)), 1)
    field = start_disp
    for sweep in range(SWEEPS):
        padded = extended(field, (("gx", 1), ("gy", 2), ("gz", 3)), 1)
        padded = padded.at[:, 1:-1, 1:-1, 0].add(ghost)
        field = relax(padded, padded_k)
    return (surface, field)


def solution(mesh):
    in_specs = (
        P(("gx", "gy", "gz"), None),
        P(("gx", "gy", "gz"), None),
        P(("gx", "gy", "gz"), None),
        P(("gx", "gy", "gz"), None),
        P(("gx", "gy", "gz"), None),
        P(("gx", "gy", "gz"), None),
        P(("gx", "gy", "gz"), None),
        P(("gx", "gy", "gz")),
        P(("gx", "gy", "gz")),
        P("gx", "gy"),
        P(None, "gx", "gy"),
        P("gx", "gy", "gz"),
        P(None, "gx", "gy", "gz"),
    )
    out_specs = (P(("gx", "gy", "gz"), None), P(None, "gx", "gy", "gz"))
    return jax.shard_map(local, mesh=mesh, in_specs=in_specs, out_specs=out_specs, check_vma=False)
```

profile of v0, /device:TPU:1, one launch (start us, length us, event | category | flops | bytes accessed | tf_op | source)
XLA Modules:
  0.0 575.2 jit_solution(4121488786621898243)
XLA Ops:
  4.2 5.3 scatter_fusion
  9.6 6.4 %all-to-all-start = ((f32[4,1,16]{2,1,0:T(1,128)}), f32[4,1,16]{2,1,0:T(1,128)S(1)}, u32[]{:S(2)}, u32[]{:S(2)}) async-start(f32[4,1,16]{2,1,0:T(1,128)} %bitcast.4), calls=%async_computation | async-start | bytes 4096 | tf_op jit(solution)/shard_map/all_to_all | solution.py:132
  45.5 5.5 collective-permute-start.11
  58.1 5.3 collective-permute-start.3
  65.4 57.0 %scatter_custom_fusion.2 = f32[1024]{0:T(1024)S(1)} fusion(s32[8192]{0:T(1024)S(1)} %bitcast.37, f32[8192]{0:T(1024)S(1)} %bitcast.42, f32[]{:T(128)} %constant.159.clone.1), kind=kCustom, calls=%fused_computation.201 | custom fusion | flops 8192 | bytes 4100 | tf_op jit(solution)/shard_map/scatter-add | solution.py:63
  122.5 57.0 %scatter_custom_fusion.4 = f32[1024]{0:T(1024)S(1)} fusion(s32[8192]{0:T(1024)S(1)} %bitcast.38, f32[8192]{0:T(1024)S(1)} %bitcast.41, f32[]{:T(128)} %constant.159.clone.1), kind=kCustom, calls=%fused_computation.197 | custom fusion | flops 8192 | bytes 4100 | tf_op jit(solution)/shard_map/scatter-add | solution.py:66
  179.5 57.0 %scatter_custom_fusion.3 = f32[1024]{0:T(1024)S(1)} fusion(s32[8192]{0:T(1024)S(1)} %bitcast.35, f32[8192]{0:T(1024)S(1)} %bitcast.40, f32[]{:T(128)} %constant.159.clone.1), kind=kCustom, calls=%fused_computation.199 | custom fusion | flops 8192 | bytes 4100 | tf_op jit(solution)/shard_map/scatter-add | solution.py:65
  236.5 57.0 %scatter_custom_fusion.5 = f32[1024]{0:T(1024)S(1)} fusion(s32[8192]{0:T(1024)S(1)} %bitcast.36, f32[8192]{0:T(1024)S(1)} %bitcast.39, f32[]{:T(128)} %constant.159.clone.1), kind=kCustom, calls=%fused_computation.195 | custom fusion | flops 8192 | bytes 4100 | tf_op jit(solution)/shard_map/scatter-add | solution.py:68
  293.5 22.5 %psum.7 = f32[2,1024]{1,0:T(2,128)S(1)} all-reduce(f32[2,1024]{1,0:T(2,128)S(1)} %pad_maximum_fusion.29), channel_id=1, replica_groups=mesh['gx'=8,'gy'=4,'gz'=8] {'gz'}, use_global_device_ids=true, to_apply=%region_8.9 | all-reduce | flops 2048 | bytes 16384 | tf_op jit(solution)/shard_map/psum | solution.py:137
  337.8 6.8 %pad_maximum_fusion = f32[3,34,34,130]{3,2,1,0:T(8,128)} fusion(f32[3,34,34,1]{3,2,1,0:T(8,128)} %copy.142, f32[3,34,1,128]{3,2,1,0:T(1,128)S(1)} %collective-permute-done.4, f32[3,34,32,128]{3,2,1,0:T(8,128)} %copy-done.3, f32[3,34,1,128]{3,2,1,0:T(1,128)S(1)} %collective-permute-done.3, f32[3,34,34,1]{3,2,1,0:T(8,128)} %copy.141), kind=kLoop, calls=%fused_computation.6 | loop fusion | flops 1803360 | bytes 3606720 | tf_op jit(solution)/shard_map/concatenate | solution.py:29
  344.7 8.8 %scatter-add.52 = f32[3,34,34,130]{3,2,1,0:T(8,128)} dynamic-update-slice(f32[3,34,34,130]{3,2,1,0:T(8,128)} %pad_maximum_fusion, f32[3,32,32,1]{3,2,1,0:T(8,128)S(1)} %copy.145, s32[]{:T(128)} %constant.160.clone.1, s32[]{:T(128)} %constant.166.clone.1, s32[]{:T(128)} %constant.166.clone.1, s32[]{:T(128)} %constant.160.clone.1) | dynamic-update-slice | bytes 24580 | tf_op jit(solution)/shard_map/scatter-add | solution.py:147
  353.5 9.9 %fusion.19 = f32[3,32,32,128]{3,2,1,0:T(8,128)S(1)} fusion(f32[3,34,34,130]{3,2,1,0:T(8,128)} %scatter-add.52, f32[32,32,128]{2,1,0:T(8,128)S(1)} %get-tuple-element.52, f32[32,32,128]{2,1,0:T(8,128)} %get-tuple-element.58, f32[32,32,128]{2,1,0:T(8,128)} %get-tuple-element.57, f32[32,32,128]{2,1,0:T(8,128)} %get-tuple-element.56, ...), kind=kLoop, calls=%fused_computation.52 | loop fusion | flops 4718592 | bytes 14680064 | tf_op jit(solution)/shard_map/div | solution.py:94
  373.8 9.9 %collective-permute-start.14 = (f32[3,34,1,128]{3,2,1,0:T(1,128)S(1)}, f32[3,34,1,128]{3,2,1,0:T(1,128)S(1)}, u32[]{:S(2)}, u32[]{:S(2)}) collective-permute-start(f32[3,34,1,128]{3,2,1,0:T(1,128)S(1)} %get-tuple-element.73), channel_id=1, source_target_pairs={{0,8},{8,16},{16,24},{1,9},{9,17},{17,25},{2,10},{10,18},{18,26},{... | collective-permute-start | bytes 156680 | tf_op jit(solution)/shard_map/ppermute | solution.py:25
  411.3 7.0 %pad_maximum_fusion.1 = f32[3,34,34,130]{3,2,1,0:T(8,128)} fusion(f32[3,34,34,1]{3,2,1,0:T(8,128)} %copy.159, f32[3,34,1,128]{3,2,1,0:T(1,128)S(1)} %collective-permute-done.15, f32[3,1,32,128]{3,2,1,0:T(8,128)S(1)} %collective-permute-done.13, f32[3,32,32,128]{3,2,1,0:T(8,128)S(1)} %fusion.19, f32[3,1,32,128]{3,2,1,0:T(8,128)S(1)} %collective-permute-done.12, ...), kind=kLoop, calls=%fused_computation.7 | loop fusion | flops 2705040 | bytes 3606720 | tf_op jit(solution)/shard_map/concatenate | solution.py:29
  418.3 9.3 %scatter-add.53 = f32[3,34,34,130]{3,2,1,0:T(8,128)} dynamic-update-slice(f32[3,34,34,130]{3,2,1,0:T(8,128)} %pad_maximum_fusion.1, f32[3,32,32,1]{3,2,1,0:T(8,128)} %copy.160, s32[]{:T(128)} %constant.160.clone.1, s32[]{:T(128)} %constant.166.clone.1, s32[]{:T(128)} %constant.166.clone.1, s32[]{:T(128)} %constant.160.clone.1) | dynamic-update-slice | bytes 24580 | tf_op jit(solution)/shard_map/scatter-add | solution.py:147
  427.6 9.6 %fusion.13 = f32[3,32,32,128]{3,2,1,0:T(8,128)S(1)} fusion(f32[3,34,34,130]{3,2,1,0:T(8,128)} %scatter-add.53, f32[32,32,128]{2,1,0:T(8,128)S(1)} %get-tuple-element.52, f32[32,32,128]{2,1,0:T(8,128)} %get-tuple-element.58, f32[32,32,128]{2,1,0:T(8,128)} %get-tuple-element.57, f32[32,32,128]{2,1,0:T(8,128)} %get-tuple-element.56, ...), kind=kLoop, calls=%fused_computation.40 | loop fusion | flops 4718592 | bytes 14680064 | tf_op jit(solution)/shard_map/div | solution.py:94
  437.3 4.9 collective-permute-start.18
  443.5 5.1 collective-permute-done.19
  480.1 7.0 %pad_maximum_fusion.2 = f32[3,34,34,130]{3,2,1,0:T(8,128)} fusion(f32[3,34,34,1]{3,2,1,0:T(8,128)} %copy.164, f32[3,34,1,128]{3,2,1,0:T(1,128)S(1)} %collective-permute-done.21, f32[3,1,32,128]{3,2,1,0:T(8,128)S(1)} %collective-permute-done.19, f32[3,32,32,128]{3,2,1,0:T(8,128)S(1)} %fusion.13, f32[3,1,32,128]{3,2,1,0:T(8,128)S(1)} %collective-permute-done.18, ...), kind=kLoop, calls=%fused_computation.8 | loop fusion | flops 2705040 | bytes 3606720 | tf_op jit(solution)/shard_map/concatenate | solution.py:29
  487.1 9.3 %scatter-add.54 = f32[3,34,34,130]{3,2,1,0:T(8,128)} dynamic-update-slice(f32[3,34,34,130]{3,2,1,0:T(8,128)} %pad_maximum_fusion.2, f32[3,32,32,1]{3,2,1,0:T(8,128)} %copy.165, s32[]{:T(128)} %constant.160.clone.1, s32[]{:T(128)} %constant.166.clone.1, s32[]{:T(128)} %constant.166.clone.1, s32[]{:T(128)} %constant.160.clone.1) | dynamic-update-slice | bytes 24580 | tf_op jit(solution)/shard_map/scatter-add | solution.py:147
  496.4 9.6 %fusion.7 = f32[3,32,32,128]{3,2,1,0:T(8,128)S(1)} fusion(f32[3,34,34,130]{3,2,1,0:T(8,128)} %scatter-add.54, f32[32,32,128]{2,1,0:T(8,128)S(1)} %get-tuple-element.52, f32[32,32,128]{2,1,0:T(8,128)} %get-tuple-element.58, f32[32,32,128]{2,1,0:T(8,128)} %get-tuple-element.57, f32[32,32,128]{2,1,0:T(8,128)} %get-tuple-element.56, ...), kind=kLoop, calls=%fused_computation.28 | loop fusion | flops 4718592 | bytes 14680064 | tf_op jit(solution)/shard_map/div | solution.py:94
  548.3 7.0 %pad_maximum_fusion.3 = f32[3,34,34,130]{3,2,1,0:T(8,128)} fusion(f32[3,34,34,1]{3,2,1,0:T(8,128)} %copy.169, f32[3,34,1,128]{3,2,1,0:T(1,128)S(1)} %collective-permute-done.27, f32[3,1,32,128]{3,2,1,0:T(8,128)S(1)} %collective-permute-done.25, f32[3,32,32,128]{3,2,1,0:T(8,128)S(1)} %fusion.7, f32[3,1,32,128]{3,2,1,0:T(8,128)S(1)} %collective-permute-done.24, ...), kind=kLoop, calls=%fused_computation.9 | loop fusion | flops 2705040 | bytes 3606720 | tf_op jit(solution)/shard_map/concatenate | solution.py:29
  555.3 9.4 %scatter-add.55 = f32[3,34,34,130]{3,2,1,0:T(8,128)} dynamic-update-slice(f32[3,34,34,130]{3,2,1,0:T(8,128)} %pad_maximum_fusion.3, f32[3,32,32,1]{3,2,1,0:T(8,128)} %copy.170, s32[]{:T(128)} %constant.160.clone.1, s32[]{:T(128)} %constant.166.clone.1, s32[]{:T(128)} %constant.166.clone.1, s32[]{:T(128)} %constant.160.clone.1) | dynamic-update-slice | bytes 24580 | tf_op jit(solution)/shard_map/scatter-add | solution.py:147
  564.8 10.2 %fusion.1 = f32[3,32,32,128]{3,2,1,0:T(8,128)} fusion(f32[3,34,34,130]{3,2,1,0:T(8,128)} %scatter-add.55, f32[32,32,128]{2,1,0:T(8,128)S(1)} %get-tuple-element.52, f32[32,32,128]{2,1,0:T(8,128)} %get-tuple-element.58, f32[32,32,128]{2,1,0:T(8,128)S(1)} %copy-done.2, f32[32,32,128]{2,1,0:T(8,128)S(1)} %copy-done.1, f32[32,32,128]{2,1,0:T(8,128)S(1)} %copy-done, ...), kind=kLoop, calls=%fused_computation.16 | loop fusion | flops 4718592 | bytes 14680064 | tf_op jit(solution)/shard_map/div | solution.py:94
  (160 shorter events, 176.6 us)
Async XLA Ops:
  9.6 22.8 %all-to-all-start = ((f32[4,1,16]{2,1,0:T(1,128)}), f32[4,1,16]{2,1,0:T(1,128)S(1)}, u32[]{:S(2)}, u32[]{:S(2)}) async-start(f32[4,1,16]{2,1,0:T(1,128)} %bitcast.4), calls=%async_computation | async-start | bytes 4096 | tf_op jit(solution)/shard_map/all_to_all | solution.py:132
  16.8 39.8 %collective-permute-start.1 = (f32[3,1,32,128]{3,2,1,0:T(8,128)S(1)}, f32[3,1,32,128]{3,2,1,0:T(8,128)S(1)}, u32[]{:S(2)}, u32[]{:S(2)}) collective-permute-start(f32[3,1,32,128]{3,2,1,0:T(8,128)S(1)} %get-tuple-element.84), channel_id=1, source_target_pairs={{0,32},{32,64},{64,96},{96,128},{128,160},{160,192},{192,224},{1,3... | collective-permute-start | bytes 147464 | tf_op jit(solution)/shard_map/ppermute | solution.py:25
  18.6 38.2 %collective-permute-start.2 = (f32[3,1,32,128]{3,2,1,0:T(8,128)S(1)}, f32[3,1,32,128]{3,2,1,0:T(8,128)S(1)}, u32[]{:S(2)}, u32[]{:S(2)}) collective-permute-start(f32[3,1,32,128]{3,2,1,0:T(8,128)S(1)} %get-tuple-element.83), channel_id=1, source_target_pairs={{32,0},{64,32},{96,64},{128,96},{160,128},{192,160},{224,192},{33,... | collective-permute-start | bytes 147464 | tf_op jit(solution)/shard_map/ppermute | solution.py:28
  20.7 15.8 %collective-permute-start.7 = (f32[1,32,128]{2,1,0:T(8,128)S(1)}, f32[1,32,128]{2,1,0:T(8,128)S(1)}, u32[]{:S(2)}, u32[]{:S(2)}) collective-permute-start(f32[1,32,128]{2,1,0:T(8,128)S(1)} %get-tuple-element.90), channel_id=1, source_target_pairs={{0,32},{32,64},{64,96},{96,128},{128,160},{160,192},{192,224},{1,3... | collective-permute-start | bytes 49160 | tf_op jit(solution)/shard_map/ppermute | solution.py:25
  24.8 11.7 %collective-permute-start = (f32[1,32,128]{2,1,0:T(8,128)S(1)}, f32[1,32,128]{2,1,0:T(8,128)S(1)}, u32[]{:S(2)}, u32[]{:S(2)}) collective-permute-start(f32[1,32,128]{2,1,0:T(8,128)S(1)} %get-tuple-element.89), channel_id=1, source_target_pairs={{32,0},{64,32},{96,64},{128,96},{160,128},{192,160},{224,192},{33,... | collective-permute-start | bytes 49160 | tf_op jit(solution)/shard_map/ppermute | solution.py:28
  32.3 33.0 %all-to-all-start.1 = ((f32[4,16,4,128]{3,2,1,0:T(4,128)}), f32[4,16,4,128]{3,2,1,0:T(4,128)S(1)}, u32[]{:S(2)}, u32[]{:S(2)}) async-start(f32[4,16,4,128]{3,2,1,0:T(4,128)} %scatter_fusion.1), calls=%async_computation.1 | async-start | bytes 262144 | tf_op jit(solution)/shard_map/all_to_all | solution.py:131
  43.8 7.4 %collective-permute-start.10 = (f32[34,34,1]{1,0,2:T(8,128)S(1)}, f32[34,34,1]{1,0,2:T(8,128)S(1)}, u32[]{:S(2)}, u32[]{:S(2)}) collective-permute-start(f32[34,34,1]{1,0,2:T(8,128)S(1)} %copy.152), channel_id=1, source_target_pairs={{1,0},{2,1},{3,2},{4,3},{5,4},{6,5},{7,6},{9,8},{10,9},{11,10},{12... | collective-permute-start | bytes 13880 | tf_op jit(solution)/shard_map/ppermute | solution.py:28
  45.5 6.4 %collective-permute-start.11 = (f32[34,34,1]{1,0,2:T(8,128)S(1)}, f32[34,34,1]{1,0,2:T(8,128)S(1)}, u32[]{:S(2)}, u32[]{:S(2)}) collective-permute-start(f32[34,34,1]{1,0,2:T(8,128)S(1)} %copy.154), channel_id=1, source_target_pairs={{0,1},{1,2},{2,3},{3,4},{4,5},{5,6},{6,7},{8,9},{9,10},{10,11},{11... | collective-permute-start | bytes 13880 | tf_op jit(solution)/shard_map/ppermute | solution.py:25
  58.1 258.0 %collective-permute-start.3 = (f32[3,34,1,128]{3,2,1,0:T(1,128)S(1)}, f32[3,34,1,128]{3,2,1,0:T(1,128)S(1)}, u32[]{:S(2)}, u32[]{:S(2)}) collective-permute-start(f32[3,34,1,128]{3,2,1,0:T(1,128)S(1)} %get-tuple-element.75), channel_id=1, source_target_pairs={{0,8},{8,16},{16,24},{1,9},{9,17},{17,25},{2,10},{10,18},{18,26},{... | collective-permute-start | bytes 156680 | tf_op jit(solution)/shard_map/ppermute | solution.py:25
  63.4 252.7 %collective-permute-start.4 = (f32[3,34,1,128]{3,2,1,0:T(1,128)S(1)}, f32[3,34,1,128]{3,2,1,0:T(1,128)S(1)}, u32[]{:S(2)}, u32[]{:S(2)}) collective-permute-start(f32[3,34,1,128]{3,2,1,0:T(1,128)S(1)} %get-tuple-element.76), channel_id=1, source_target_pairs={{8,0},{16,8},{24,16},{9,1},{17,9},{25,17},{10,2},{18,10},{26,18},{... | collective-permute-start | bytes 156680 | tf_op jit(solution)/shard_map/ppermute | solution.py:28
  323.0 6.7 %collective-permute-start.5 = (f32[3,34,34,1]{2,1,0,3:T(8,128)S(1)}, f32[3,34,34,1]{2,1,0,3:T(8,128)S(1)}, u32[]{:S(2)}, u32[]{:S(2)}) collective-permute-start(f32[3,34,34,1]{2,1,0,3:T(8,128)S(1)} %copy.171), channel_id=1, source_target_pairs={{0,1},{1,2},{2,3},{3,4},{4,5},{5,6},{6,7},{8,9},{9,10},{10,11},{11... | collective-permute-start | bytes 41624 | tf_op jit(solution)/shard_map/ppermute | solution.py:25
  328.4 6.5 %collective-permute-start.6 = (f32[3,34,34,1]{2,3,1,0:T(1,128)S(1)}, f32[3,34,34,1]{2,3,1,0:T(1,128)}, u32[]{:S(2)}, u32[]{:S(2)}) collective-permute-start(f32[3,34,34,1]{2,3,1,0:T(1,128)S(1)} %copy.172), channel_id=1, source_target_pairs={{1,0},{2,1},{3,2},{4,3},{5,4},{6,5},{7,6},{9,8},{10,9},{11,10},{12... | collective-permute-start | bytes 41624 | tf_op jit(solution)/shard_map/ppermute | solution.py:28
  367.7 6.0 %collective-permute-start.13 = (f32[3,1,32,128]{3,2,1,0:T(8,128)S(1)}, f32[3,1,32,128]{3,2,1,0:T(8,128)S(1)}, u32[]{:S(2)}, u32[]{:S(2)}) collective-permute-start(f32[3,1,32,128]{3,2,1,0:T(8,128)S(1)} %get-tuple-element.82), channel_id=1, source_target_pairs={{32,0},{64,32},{96,64},{128,96},{160,128},{192,160},{224,192},{33,... | collective-permute-start | bytes 147464 | tf_op jit(solution)/shard_map/ppermute | solution.py:28
  373.8 11.9 %collective-permute-start.14 = (f32[3,34,1,128]{3,2,1,0:T(1,128)S(1)}, f32[3,34,1,128]{3,2,1,0:T(1,128)S(1)}, u32[]{:S(2)}, u32[]{:S(2)}) collective-permute-start(f32[3,34,1,128]{3,2,1,0:T(1,128)S(1)} %get-tuple-element.73), channel_id=1, source_target_pairs={{0,8},{8,16},{16,24},{1,9},{9,17},{17,25},{2,10},{10,18},{18,26},{... | collective-permute-start | bytes 156680 | tf_op jit(solution)/shard_map/ppermute | solution.py:25
  394.7 8.5 %collective-permute-start.16 = (f32[3,34,34,1]{2,1,0,3:T(8,128)S(1)}, f32[3,34,34,1]{2,1,0,3:T(8,128)S(1)}, u32[]{:S(2)}, u32[]{:S(2)}) collective-permute-start(f32[3,34,34,1]{2,1,0,3:T(8,128)S(1)} %copy.175), channel_id=1, source_target_pairs={{0,1},{1,2},{2,3},{3,4},{4,5},{5,6},{6,7},{8,9},{9,10},{10,11},{11... | collective-permute-start | bytes 41624 | tf_op jit(solution)/shard_map/ppermute | solution.py:25
  401.7 6.7 %collective-permute-start.17 = (f32[3,34,34,1]{2,3,1,0:T(1,128)}, f32[3,34,34,1]{2,3,1,0:T(1,128)}, u32[]{:S(2)}, u32[]{:S(2)}) collective-permute-start(f32[3,34,34,1]{2,3,1,0:T(1,128)} %copy.176), channel_id=1, source_target_pairs={{1,0},{2,1},{3,2},{4,3},{5,4},{6,5},{7,6},{9,8},{10,9},{11,10},{12... | collective-permute-start | bytes 41624 | tf_op jit(solution)/shard_map/ppermute | solution.py:28
  437.3 6.2 %collective-permute-start.18 = (f32[3,1,32,128]{3,2,1,0:T(8,128)S(1)}, f32[3,1,32,128]{3,2,1,0:T(8,128)S(1)}, u32[]{:S(2)}, u32[]{:S(2)}) collective-permute-start(f32[3,1,32,128]{3,2,1,0:T(8,128)S(1)} %get-tuple-element.79), channel_id=1, source_target_pairs={{0,32},{32,64},{64,96},{96,128},{128,160},{160,192},{192,224},{1,3... | collective-permute-start | bytes 147464 | tf_op jit(solution)/shard_map/ppermute | solution.py:25
  442.1 6.4 %collective-permute-start.19 = (f32[3,1,32,128]{3,2,1,0:T(8,128)S(1)}, f32[3,1,32,128]{3,2,1,0:T(8,128)S(1)}, u32[]{:S(2)}, u32[]{:S(2)}) collective-permute-start(f32[3,1,32,128]{3,2,1,0:T(8,128)S(1)} %get-tuple-element.80), channel_id=1, source_target_pairs={{32,0},{64,32},{96,64},{128,96},{160,128},{192,160},{224,192},{33,... | collective-permute-start | bytes 147464 | tf_op jit(solution)/shard_map/ppermute | solution.py:28
  463.3 8.7 %collective-permute-start.22 = (f32[3,34,34,1]{2,1,0,3:T(8,128)S(1)}, f32[3,34,34,1]{2,1,0,3:T(8,128)S(1)}, u32[]{:S(2)}, u32[]{:S(2)}) collective-permute-start(f32[3,34,34,1]{2,1,0,3:T(8,128)S(1)} %copy.177), channel_id=1, source_target_pairs={{0,1},{1,2},{2,3},{3,4},{4,5},{5,6},{6,7},{8,9},{9,10},{10,11},{11... | collective-permute-start | bytes 41624 | tf_op jit(solution)/shard_map/ppermute | solution.py:25
  470.5 6.7 %collective-permute-start.23 = (f32[3,34,34,1]{2,3,1,0:T(1,128)}, f32[3,34,34,1]{2,3,1,0:T(1,128)}, u32[]{:S(2)}, u32[]{:S(2)}) collective-permute-start(f32[3,34,34,1]{2,3,1,0:T(1,128)} %copy.178), channel_id=1, source_target_pairs={{1,0},{2,1},{3,2},{4,3},{5,4},{6,5},{7,6},{9,8},{10,9},{11,10},{12... | collective-permute-start | bytes 41624 | tf_op jit(solution)/shard_map/ppermute | solution.py:28
  506.1 6.2 %collective-permute-start.24 = (f32[3,1,32,128]{3,2,1,0:T(8,128)S(1)}, f32[3,1,32,128]{3,2,1,0:T(8,128)S(1)}, u32[]{:S(2)}, u32[]{:S(2)}) collective-permute-start(f32[3,1,32,128]{3,2,1,0:T(8,128)S(1)} %get-tuple-element.77), channel_id=1, source_target_pairs={{0,32},{32,64},{64,96},{96,128},{128,160},{160,192},{192,224},{1,3... | collective-permute-start | bytes 147464 | tf_op jit(solution)/shard_map/ppermute | solution.py:25
  516.2 5.7 collective-permute-start.26
  530.9 9.3 %collective-permute-start.28 = (f32[3,34,34,1]{2,1,0,3:T(8,128)S(1)}, f32[3,34,34,1]{2,1,0,3:T(8,128)S(1)}, u32[]{:S(2)}, u32[]{:S(2)}) collective-permute-start(f32[3,34,34,1]{2,1,0,3:T(8,128)S(1)} %copy.179), channel_id=1, source_target_pairs={{0,1},{1,2},{2,3},{3,4},{4,5},{5,6},{6,7},{8,9},{9,10},{10,11},{11... | collective-permute-start | bytes 41624 | tf_op jit(solution)/shard_map/ppermute | solution.py:25
  538.7 6.7 %collective-permute-start.29 = (f32[3,34,34,1]{2,3,1,0:T(1,128)}, f32[3,34,34,1]{2,3,1,0:T(1,128)}, u32[]{:S(2)}, u32[]{:S(2)}) collective-permute-start(f32[3,34,34,1]{2,3,1,0:T(1,128)} %copy.180), channel_id=1, source_target_pairs={{1,0},{2,1},{3,2},{4,3},{5,4},{6,5},{7,6},{9,8},{10,9},{11,10},{12... | collective-permute-start | bytes 41624 | tf_op jit(solution)/shard_map/ppermute | solution.py:28
  (18 other events, 149.9 us)
where the time goes:
time: 587 us; the launch traced here: 575 us
  other arithmetic  308 us (52%)
  local copies, waits for them, and re-layouts  111 us (19%)
  starting transfers between devices  101 us (17%)
  waiting for transfers between devices  30.9 us (5%)
  blocking collectives  22.5 us (4%)
    ppermute x15, starting transfers between devices, extended(): lax.ppermute(lax.slice_in_dim(block, block.shape[dim] - width, None, axis...  67.7 us
    scatter-add x1, other arithmetic, deposit(): jax.ops.segment_sum(terms[:, 0].reshape(-1), first, num_segments=segments)  57 us
    scatter-add x1, other arithmetic, deposit(): jax.ops.segment_sum(terms[:, 2].reshape(-1), first, num_segments=segments)  57 us
    scatter-add x1, other arithmetic, deposit(): jax.ops.segment_sum(terms[:, 1].reshape(-1), second, num_segments=segments)  57 us
    scatter-add x1, other arithmetic, deposit(): jax.ops.segment_sum(terms[:, 3].reshape(-1), second, num_segments=segments)  57 us
    div x4, other arithmetic, relax(): return total / weight  39.4 us
    scatter-add x4, local copies, waits for them, and re-layouts, local(): padded = padded.at[:, 1:-1, 1:-1, 0].add(ghost)  36.7 us
    concatenate x9, other arithmetic, extended(): block = jnp.concatenate([low, block, high], axis=dim)  30.6 us
  transfers between devices with their start and end apart: 32, of which 12 were waited for; matrix products, arithmetic and copies ran while one was open for 47% of the time, Pallas kernels for 0%

commit v1 on v0

v1 whole, which is shorter than its diff:
```python
import jax
import jax.numpy as jnp
from jax import lax
from jax.experimental import pallas as pl
from jax.experimental.pallas import tpu as pltpu
from jax.sharding import PartitionSpec as P

NEWTON = 6
SWEEPS = 4
MESH = pl.DeviceIdType.MESH
F32 = jnp.float32
SIZES = {"gx": 8, "gy": 4, "gz": 8}
BX = 32
EXT = 40
FLAT = 48 * 128

arrhenius_scale = 0.5
activation = 3.0
blowing = 0.5
heat_release = 0.3
radiation = 0.05
conduction = 0.5
time_step = 1.5


def ablation_rate(surface):
    return arrhenius_scale * jnp.exp(activation * (1.0 - 1.0 / surface))


def balance_step(surface, recovery_temp, film_coeff, emissivity, back_temp):
    ablate = ablation_rate(surface)
    film = film_coeff * film_coeff / (film_coeff + blowing * ablate)
    cubed = surface * surface * surface
    imbalance = (
        film * (recovery_temp - surface)
        + heat_release * ablate
        - radiation * emissivity * (cubed * surface)
        - conduction * (surface - back_temp)
    )
    slope = film + 4.0 * radiation * emissivity * cubed + conduction
    return surface + imbalance / slope


def lanes(shape):
    return lax.broadcasted_iota(jnp.int32, shape, len(shape) - 1)


def rows(shape):
    return lax.broadcasted_iota(jnp.int32, shape, len(shape) - 2)


def place(x):
    start = (x + 16) * 136 + 4
    return start // 128 - 10, start % 128


def kernel(
    recovery_temp, film_coeff, emissivity, char_density, back_temp, stencil_frac,
    wall_owner, stencil_start, live_count, wall_mask, wall_dir, stiffness, start_disp,
    surface_out, disp_out,
    own, below, above, strip_up, strip_down, strip_from_below, strip_from_above,
    slab_up, slab_down, slab_below, slab_above, edge_send, edge_recv,
    slabs, cross_send, cross_recv,
    field_a, field_b, weights, result, thin_weights, thin, source,
    dep_send, dep_recv, ghost, ghost_side, ghost_face, ghost_corner, ghost_all,
    local_sem, send_sem, recv_sem, dep_sem,
):
    gx, gy, gz = (lax.axis_index(a) for a in ("gx", "gy", "gz"))
    position = (gx, gy, gz)
    limits = (SIZES["gx"], SIZES["gy"], SIZES["gz"])

    def there(step):
        found = None
        for p, d, n in zip(position, step, limits):
            if d != 0:
                ok = (p + d >= 0) & (p + d < n)
                found = ok if found is None else found & ok
        return found

    def target(step):
        return tuple(p + d for p, d in zip(position, step))

    def back(step):
        return tuple(-d for d in step)

    on_wall = gz == 0

    class Message:
        def __init__(self, channel, step, src, dst, walls=False):
            self.to, self.origin = there(step), there(back(step))
            if walls:
                self.to, self.origin = self.to & on_wall, self.origin & on_wall
            self.copy = pltpu.make_async_remote_copy(
                src_ref=src, dst_ref=dst, send_sem=send_sem.at[channel], recv_sem=recv_sem.at[channel],
                device_id=target(step), device_id_type=MESH,
            )

        def start(self):
            pl.when(self.to)(self.copy.start)

        def wait_recv(self):
            pl.when(self.origin)(self.copy.wait_recv)

        def wait_send(self):
            pl.when(self.to)(self.copy.wait_send)

    load_u = pltpu.make_async_copy(start_disp, own.at[0:3, :, 0:32], local_sem.at[0])
    load_k = pltpu.make_async_copy(stiffness, own.at[3, :, 0:32], local_sem.at[1])
    load_u.start()
    load_k.start()

    barrier = pltpu.get_barrier_semaphore()
    near = [(1, 0, 0), (-1, 0, 0), (0, 1, 0), (0, -1, 0), (0, 0, 1), (0, 0, -1)]
    near += [(0, a, b) for a in (1, -1) for b in (1, -1)]
    corners = [(a, b, 0) for a in (1, -1) for b in (1, -1)]
    expected = jnp.where(on_wall, 3, 4)

    def greet(step, ok):
        pl.when(ok)(lambda: pl.semaphore_signal(barrier, inc=1, device_id=target(step), device_id_type=MESH))
        return ok.astype(jnp.int32)

    for step in near:
        expected = expected + greet(step, there(step))
    for step in corners:
        expected = expected + greet(step, there(step) & on_wall)
    rank = gy * limits[2] + gz
    for y in range(limits[1]):
        for z in range(limits[2]):
            pl.when(on_wall & (rank != y * limits[2] + z))(
                lambda y=y, z=z: pl.semaphore_signal(barrier, inc=1, device_id=(gx, y, z), device_id_type=MESH)
            )

    back_t = back_temp[...]
    surface = back_t
    for _ in range(NEWTON):
        surface = balance_step(surface, recovery_temp[...], film_coeff[...], emissivity[...], back_t)
    surface_out[...] = surface
    recession = time_step * ablation_rate(surface) / char_density[...]
    shape = (32, 128)
    lane = lanes(shape)
    square = (32, 32)
    diagonal = rows(square) == lanes(square)

    def column(row):
        spread = jnp.broadcast_to(row.astype(F32), square)
        return jnp.broadcast_to(jnp.sum(jnp.where(diagonal, spread, 0.0), axis=1, keepdims=True), shape)

    starts = stencil_start[...]
    shift = column(starts & 127)
    live = lane.astype(F32) < column(live_count[...])
    upper = jnp.where(live, stencil_frac[...], 0.0)
    lower = jnp.where(live, 1.0 - stencil_frac[...], 0.0)
    shift = shift.astype(jnp.int32)
    first, second = [], []
    for low, high in ((lower * recession, upper * recession), (lower, upper)):
        moved = pltpu.roll(high, 1, axis=1)
        spread = low + jnp.where(lane >= 1, moved, 0.0)
        last = jnp.broadcast_to(moved[:, 0:1], shape)
        for bit in range(7):
            spread = jnp.where(((shift >> bit) & 1) == 1, pltpu.roll(spread, 1 << bit, axis=1), spread)
        first.append(jnp.where(lane >= shift, spread, 0.0))
        second.append(jnp.where(lane < shift, spread, jnp.where(lane == shift, last, 0.0)))
    face_row = wall_owner[...] * 8
    row_a = jnp.broadcast_to(face_row + (starts >> 7), square)
    row_b = jnp.broadcast_to(face_row + (((starts >> 7) + 1) & 7), square)

    def gathered(row, terms):
        pick = (rows(square) == row).astype(F32)
        return jnp.dot(pick, terms, precision=lax.Precision.HIGHEST, preferred_element_type=F32)

    summed = gathered(row_a, jnp.concatenate(first, axis=1)) + gathered(row_b, jnp.concatenate(second, axis=1))
    for o in range(4):
        dep_send[o, 0:8] = summed[8 * o : 8 * o + 8, 0:128]
        dep_send[o, 8:16] = summed[8 * o : 8 * o + 8, 128:256]

    tile = (8, 128)
    top = rows(tile) < 4
    load_u.wait()
    load_k.wait()
    group = lanes(shape) // 8
    inner = lanes(shape) % 8 < 4

    def pack_z(c, _):
        halves = []
        for p in range(2):
            packed = jnp.zeros(shape, F32)
            for i in range(16):
                turned = pltpu.roll(own[c, 16 * p + i, 0:32], 8 * i + 4, axis=1)
                packed = jnp.where(group == i, turned, packed)
            halves.append(packed)
        slab_up[c] = jnp.where(inner, halves[0], pltpu.roll(halves[1], 4, axis=1))
        slab_down[c] = jnp.where(inner, pltpu.roll(halves[0], 124, axis=1), halves[1])
        return 0

    lax.fori_loop(0, 4, pack_z, 0)

    def rows_down(a, b):
        return jnp.where(top, a, pltpu.roll(b, 4, axis=0))

    def rows_up(a, b):
        return jnp.where(top, pltpu.roll(b, 4, axis=0), a)

    def pack_y(x, _):
        for pair in range(2):
            a, b = 2 * pair, 2 * pair + 1
            strip_down[pair, x] = rows_down(own[a, x, 0:8], own[b, x, 0:8])
            strip_up[pair, x] = rows_up(own[a, x, 24:32], own[b, x, 24:32])
        return 0

    lax.fori_loop(0, 32, pack_y, 0)
    for pair in range(2):
        a, b = 2 * pair, 2 * pair + 1
        edge_send[0, pair] = rows_down(slab_up[a, 0:8], slab_up[b, 0:8])
        edge_send[1, pair] = rows_up(slab_up[a, 24:32], slab_up[b, 24:32])
        edge_send[2, pair] = rows_down(slab_down[a, 0:8], slab_down[b, 0:8])
        edge_send[3, pair] = rows_up(slab_down[a, 24:32], slab_down[b, 24:32])

    east, west, north, south = (1, 0, 0), (-1, 0, 0), (0, 1, 0), (0, -1, 0)
    x_far = [
        Message(0, east, start_disp.at[:, 28:32], below.at[0:3, :, 0:32]),
        Message(1, east, stiffness.at[28:32], below.at[3, :, 0:32]),
        Message(2, west, start_disp.at[:, 0:4], above.at[0:3, :, 0:32]),
        Message(3, west, stiffness.at[0:4], above.at[3, :, 0:32]),
    ]
    y_far = [Message(4, north, strip_up, strip_from_below), Message(5, south, strip_down, strip_from_above)]
    z_far = [
        Message(6, (0, 0, 1), slab_up, slab_below.at[:, 0:32]),
        Message(7, (0, 0, -1), slab_down, slab_above.at[:, 0:32]),
    ]
    edges = [
        Message(8, (0, -1, 1), edge_send.at[0], edge_recv.at[0]),
        Message(9, (0, 1, 1), edge_send.at[1], edge_recv.at[1]),
        Message(10, (0, -1, -1), edge_send.at[2], edge_recv.at[2]),
        Message(11, (0, 1, -1), edge_send.at[3], edge_recv.at[3]),
    ]

    pl.semaphore_wait(barrier, expected)

    def deposit_copy(y):
        ahead = lax.rem(rank - y * limits[2] + 32, 32)
        slot = jnp.maximum(ahead - 1, 0)
        copy = pltpu.make_async_remote_copy(
            src_ref=dep_send.at[y], dst_ref=dep_recv.at[slot], send_sem=send_sem.at[24 + y], recv_sem=dep_sem.at[0],
            device_id=(gx, y, 0), device_id_type=MESH,
        )
        return ahead != 0, copy

    for message in z_far + edges + y_far:
        message.start()
    for y in range(4):
        away, copy = deposit_copy(y)
        pl.when(away)(copy.start)
    for message in x_far:
        message.start()

    def clear(step, *refs):
        @pl.when(jnp.logical_not(there(step)))
        def _():
            for ref in refs:
                ref[...] = jnp.zeros(ref.shape, F32)

    clear(north, strip_from_above)
    clear(south, strip_from_below)
    clear((0, 0, -1), slab_below.at[:, 0:32])
    clear((0, 0, 1), slab_above.at[:, 0:32])
    for k, message_step in enumerate(((0, -1, 1), (0, 1, 1), (0, -1, -1), (0, 1, -1))):
        clear(back(message_step), edge_recv.at[k])
    clear(west, below.at[:, :, 0:32], below.at[:, 1:4, 32:40], cross_recv.at[0])
    clear(east, above.at[:, :, 0:32], above.at[:, 0:3, 32:40], cross_recv.at[1])
    below[:, 0, 32:40] = jnp.zeros((4, 8, 128), F32)
    above[:, 3, 32:40] = jnp.zeros((4, 8, 128), F32)

    for message in z_far + edges + y_far:
        message.wait_recv()

    def merged(from_above, from_below):
        a = jnp.where(top, from_above, from_below)
        b = pltpu.roll(jnp.where(top, from_below, from_above), 4, axis=0)
        return a, b

    def merge_y(x, _):
        for pair in range(2):
            a, b = merged(strip_from_above[pair, x], strip_from_below[pair, x])
            own[2 * pair, x, 32:40] = a
            own[2 * pair + 1, x, 32:40] = b
        return 0

    lax.fori_loop(0, 32, merge_y, 0)
    for pair in range(2):
        a, b = merged(edge_recv[0, pair], edge_recv[1, pair])
        slab_below[2 * pair, 32:40] = a
        slab_below[2 * pair + 1, 32:40] = b
        a, b = merged(edge_recv[2, pair], edge_recv[3, pair])
        slab_above[2 * pair, 32:40] = a
        slab_above[2 * pair + 1, 32:40] = b
    tall = (EXT, 128)
    tall_inner = lanes(tall) % 8 < 4
    block = lanes(tall) // 32
    up, down = jnp.zeros(tall, F32), jnp.zeros(tall, F32)
    for c in range(4):
        under, over = slab_below[c], slab_above[c]
        left = jnp.where(tall_inner, under, pltpu.roll(over, 4, axis=1))
        right = jnp.where(tall_inner, pltpu.roll(under, 124, axis=1), over)
        slabs[c, 0] = left
        slabs[c, 1] = right
        down = jnp.where(block == c, pltpu.roll(left, 32 * c, axis=1), down)
        up = jnp.where(block == c, pltpu.roll(right, (32 * c + 32) % 128, axis=1), up)
    cross_send[0] = up
    cross_send[1] = down
    x_near = [
        Message(12, east, own.at[:, 29:32, 32:40], below.at[:, 1:4, 32:40]),
        Message(13, west, own.at[:, 0:3, 32:40], above.at[:, 0:3, 32:40]),
        Message(14, east, cross_send.at[0], cross_recv.at[0]),
        Message(15, west, cross_send.at[1], cross_recv.at[1]),
    ]
    for message in x_near:
        message.start()

    @pl.when(on_wall)
    def _():
        everyone = pltpu.make_async_remote_copy(
            src_ref=dep_recv, dst_ref=dep_recv, send_sem=send_sem.at[24], recv_sem=dep_sem.at[0],
            device_id=(gx, 0, 0), device_id_type=MESH,
        )
        everyone.wait_recv()
        total = dep_send[gy]
        for k in range(31):
            total = total + dep_recv[k]
        face = total[0:8] / (1.0 + total[8:16])
        wide = (8, 256)
        acc = jnp.zeros((96, 256), F32)
        for q in range(4):
            mask = wall_mask[pl.ds(q, 8, stride=4), :].astype(F32)
            part = face[:, 32 * q : 32 * q + 32] * (-mask)
            values = jnp.concatenate([part * wall_dir[c, pl.ds(q, 8, stride=4), :] for c in range(3)], axis=1)
            pick = (lanes(wide) == 32 * rows(wide) + 8 * q + 3).astype(F32)
            acc = acc + lax.dot_general(
                values, pick, (((0,), (0,)), ((), ())), precision=lax.Precision.HIGHEST, preferred_element_type=F32
            )
        for c in range(3):
            for p in range(2):
                ghost[p, c] = acc[32 * c : 32 * c + 32, 128 * p : 128 * p + 128]

    g_side = [
        Message(16, north, ghost.at[:, :, 24:32], ghost_side.at[0], True),
        Message(17, south, ghost.at[:, :, 0:8], ghost_side.at[1], True),
    ]
    g_face = [
        Message(18, east, ghost.at[1], ghost_face.at[0], True),
        Message(19, west, ghost.at[0], ghost_face.at[1], True),
    ]
    g_corner = [
        Message(20, (1, 1, 0), ghost.at[1, :, 24:32], ghost_corner.at[0], True),
        Message(21, (1, -1, 0), ghost.at[1, :, 0:8], ghost_corner.at[1], True),
        Message(22, (-1, 1, 0), ghost.at[0, :, 24:32], ghost_corner.at[2], True),
        Message(23, (-1, -1, 0), ghost.at[0, :, 0:8], ghost_corner.at[3], True),
    ]
    g_all = g_side + g_face + g_corner
    for message in g_all:
        message.start()
    clear(south, ghost_side.at[0])
    clear(north, ghost_side.at[1])
    clear(west, ghost_face.at[0])
    clear(east, ghost_face.at[1])
    for k, step in enumerate(((1, 1, 0), (1, -1, 0), (-1, 1, 0), (-1, -1, 0))):
        clear(back(step), ghost_corner.at[k])

    for message in x_far + x_near:
        message.wait_recv()
    for c in range(4):
        low = pltpu.roll(cross_recv[0], (96 - 32 * c) % 128, axis=1)
        high = pltpu.roll(cross_recv[1], (128 - 32 * c) % 128, axis=1)
        slabs[c, 2] = jnp.where(block < 2, high, low)
    tile_lane = lanes(tile)

    def flatten(step, _):
        c, j = lax.div(step, 5), lax.rem(step, 5)

        def put(p, value):
            field_a[c, j, :, 128 * p : 128 * p + 128] = value

        def turned(ref, e, i):
            return pltpu.roll(ref[c, e, pl.ds(j, 8, stride=5), :], 8 * i + 4, axis=1)

        for p in (0, 1, 46, 47):
            put(p, jnp.zeros(tile, F32))
        for first_x, count, ref, base, s in ((-4, 4, below, -4, 2), (0, 16, own, 0, 0), (16, 16, own, 0, 1), (32, 4, above, 32, 2)):
            slab = slabs[c, s, pl.ds(j, 8, stride=5), :]
            before = None
            for x in range(first_x, first_x + count):
                p, at = place(x)
                now = turned(ref, x - base, x % 16)
                value = jnp.where(tile_lane < at, slab, now)
                if before is not None:
                    value = jnp.where(tile_lane < at - 8, before, value)
                put(p, value)
                before = now
            put(p + 1, jnp.where(tile_lane < at, before, slab))
        return 0

    lax.fori_loop(0, 20, flatten, 0)

    N = 4
    ends = tile_lane < 1, tile_lane > 126, tile_lane < 8, tile_lane >= 120

    def column_at(q):
        return pl.ds(pl.multiple_of(q * 128, 128), 128)

    def window(field, c, j, q):
        at = {k: field[c, j, :, column_at(q + k)] for k in range(-2, N + 2)}
        z_up = [pltpu.roll(at[k], 127, axis=1) for k in range(0, N + 1)]
        z_down = [pltpu.roll(at[k], 1, axis=1) for k in range(-1, N)]
        x_up = [pltpu.roll(at[k], 120, axis=1) for k in range(1, N + 2)]
        x_down = [pltpu.roll(at[k], 8, axis=1) for k in range(-2, N - 1)]
        return [
            (
                at[k],
                jnp.where(ends[3], x_up[k + 1], x_up[k]),
                jnp.where(ends[2], x_down[k], x_down[k + 1]),
                jnp.where(ends[1], z_up[k + 1], z_up[k]),
                jnp.where(ends[0], z_down[k], z_down[k + 1]),
            )
            for k in range(N)
        ]

    def part(field, c, j, q):
        if j == 5:
            return pltpu.roll(field[c, 0, :, column_at(q)], 7, axis=0)
        if j == -1:
            return pltpu.roll(field[c, 4, :, column_at(q)], 1, axis=0)
        return field[c, j, :, column_at(q)]

    def weigh(step, _):
        q = 2 + step * N
        for j in range(5):
            for k, (centre, xp, xm, zp, zm) in enumerate(window(field_a, 3, j, q)):
                sides = (xp, xm, part(field_a, 3, j + 1, q + k), part(field_a, 3, j - 1, q + k), zp, zm)
                weight = 6.0 * centre
                for side in sides:
                    weight = weight + side
                inverse = jnp.where(centre > 0.0, 1.0 / weight, 0.0)
                for n, side in enumerate(sides):
                    weights[n, j, :, column_at(q + k)] = (centre + side) * inverse
        return 0

    lax.fori_loop(0, 44 // N, weigh, 0)

    for c in range(3):
        for j in range(5):
            field_b[c, j, :, 0:384] = jnp.zeros((8, 384), F32)
            field_b[c, j, :, 5760:6144] = jnp.zeros((8, 384), F32)
    for sweep, (start, end) in enumerate(((2, 46), (4, 44), (5, 43), (7, 41))):
        src, dst = (field_a, field_b) if sweep % 2 == 0 else (field_b, field_a)

        def relax(step, _, src=src, dst=dst, start=start):
            q = start + step * N
            for j in range(5):
                around = [window(src, c, j, q) for c in range(3)]
                for k in range(N):
                    w = [weights[n, j, :, column_at(q + k)] for n in range(6)]
                    for c in range(3):
                        _, xp, xm, zp, zm = around[c][k]
                        total = w[0] * xp + w[1] * xm
                        total = total + (w[2] * part(src, c, j + 1, q + k) + w[3] * part(src, c, j - 1, q + k))
                        dst[c, j, :, column_at(q + k)] = total + (w[4] * zp + w[5] * zm)
            return 0

        lax.fori_loop(0, -(-(end - start) // N), relax, 0)

    thin[...] = jnp.zeros(thin.shape, F32)

    @pl.when(on_wall)
    def _():
        for message in g_all:
            message.wait_recv()
        for c in range(3):
            for p in range(2):
                ghost_all[c, p, 0:32] = ghost[p, c]
                ghost_all[c, p, 32:40] = jnp.where(top, ghost_side[1, p, c], ghost_side[0, p, c])
            ghost_all[c, 2, 0:32] = jnp.where(lane < 64, ghost_face[1, c], ghost_face[0, c])
            left = tile_lane < 64
            over = jnp.where(left, ghost_corner[3, c], ghost_corner[1, c])
            under = jnp.where(left, ghost_corner[2, c], ghost_corner[0, c])
            ghost_all[c, 2, 32:40] = jnp.where(top, over, under)
        main = tile_lane % 8 >= 4
        octet = tile_lane // 8

        def gather(step, _):
            n, j = lax.div(step, 5), lax.rem(step, 5)
            for s, xs in ((0, range(16)), (1, range(16, 32)), (2, (-4, -3, -2, -1, 32, 33, 34, 35))):
                value = jnp.zeros(tile, F32)
                for x in xs:
                    p, _ = place(x)
                    value = jnp.where(main & (octet == x % 16), weights[n, j, :, 128 * p : 128 * p + 128], value)
                thin_weights[n, j, :, 128 * s : 128 * s + 128] = value
            return 0

        lax.fori_loop(0, 30, gather, 0)
        span = (8, 384)
        for c in range(3):
            for j in range(5):
                wall = jnp.concatenate([ghost_all[c, s, pl.ds(j, 8, stride=5), :] for s in range(3)], axis=1)
                value = thin_weights[5, j] * pltpu.roll(wall, 1, axis=1)
                source[c, j] = value
                thin[0, c, j] = value
        for sweep in range(SWEEPS - 1):
            src, dst = sweep % 2, (sweep + 1) % 2

            def step_thin(c, _, src=src, dst=dst):
                for j in range(5):
                    here = thin[src, c, j]
                    after = thin[src, c, j + 1] if j < 4 else pltpu.roll(thin[src, c, 0], 7, axis=0)
                    prior = thin[src, c, j - 1] if j > 0 else pltpu.roll(thin[src, c, 4], 1, axis=0)
                    total = source[c, j] + thin_weights[0, j] * pltpu.roll(here, 384 - 8, axis=1)
                    total = total + thin_weights[1, j] * pltpu.roll(here, 8, axis=1)
                    total = total + thin_weights[2, j] * after + thin_weights[3, j] * prior
                    total = total + thin_weights[4, j] * pltpu.roll(here, 383, axis=1)
                    thin[dst, c, j] = total + thin_weights[5, j] * pltpu.roll(here, 1, axis=1)
                return 0

            lax.fori_loop(0, 3, step_thin, 0)

    thin_final = (SWEEPS - 1) % 2
    outs = []
    for c in range(3):

        def unflatten(j, _, c=c):
            for s in range(2):
                extra = thin[thin_final, c, j, :, 128 * s : 128 * s + 128]
                for x in range(16 * s, 16 * s + 16):
                    p, at = place(x)
                    low = field_a[c, j, :, 128 * p : 128 * p + 128]
                    low = low + jnp.where(tile_lane < at + 4, extra, 0.0)
                    high = field_a[c, j, :, 128 * p + 128 : 128 * p + 256]
                    value = pltpu.roll(jnp.where(tile_lane >= at, low, high), 128 - at, axis=1)
                    result[c, x, pl.ds(j, 8, stride=5), :] = value
            return 0

        lax.fori_loop(0, 5, unflatten, 0)
        copy = pltpu.make_async_copy(result.at[c, :, 0:32], disp_out.at[c], local_sem.at[2 + c])
        copy.start()
        outs.append(copy)

    for message in x_far + y_far + z_far + edges + x_near + g_all:
        message.wait_send()
    for y in range(4):
        away, copy = deposit_copy(y)
        pl.when(away)(copy.wait_send)
    for copy in outs:
        copy.wait()


def local(
    recovery_temp, film_coeff, emissivity, char_density, back_temp, stencil_frac,
    wall_owner, stencil_start, live_count, wall_mask, wall_dir, stiffness, start_disp,
):
    vmem = pl.BlockSpec(memory_space=pltpu.VMEM)
    hbm = pl.BlockSpec(memory_space=pltpu.HBM)
    scratch = [
        (4, 32, EXT, 128),
        (4, 4, EXT, 128),
        (4, 4, EXT, 128),
        (2, 32, 8, 128),
        (2, 32, 8, 128),
        (2, 32, 8, 128),
        (2, 32, 8, 128),
        (4, 32, 128),
        (4, 32, 128),
        (4, EXT, 128),
        (4, EXT, 128),
        (4, 2, 8, 128),
        (4, 2, 8, 128),
        (4, 3, EXT, 128),
        (2, EXT, 128),
        (2, EXT, 128),
        (4, 5, 8, FLAT),
        (3, 5, 8, FLAT),
        (6, 5, 8, FLAT),
        (3, 32, EXT, 128),
        (6, 5, 8, 384),
        (2, 3, 5, 8, 384),
        (3, 5, 8, 384),
        (4, 16, 128),
        (31, 16, 128),
        (2, 3, 32, 128),
        (2, 2, 3, 8, 128),
        (2, 3, 32, 128),
        (4, 3, 8, 128),
        (3, 3, EXT, 128),
    ]
    return pl.pallas_call(
        kernel,
        out_shape=(
            jax.ShapeDtypeStruct(back_temp.shape, F32),
            jax.ShapeDtypeStruct(start_disp.shape, F32),
        ),
        in_specs=[vmem] * 11 + [hbm] * 2,
        out_specs=(vmem, hbm),
        scratch_shapes=[pltpu.VMEM(s, F32) for s in scratch]
        + [
            pltpu.SemaphoreType.DMA((5,)),
            pltpu.SemaphoreType.DMA((28,)),
            pltpu.SemaphoreType.DMA((24,)),
            pltpu.SemaphoreType.DMA((1,)),
        ],
        compiler_params=pltpu.CompilerParams(collective_id=0, has_side_effects=True, vmem_limit_bytes=60 << 20),
    )(
        recovery_temp, film_coeff, emissivity, char_density, back_temp, stencil_frac,
        wall_owner.reshape(1, 32), stencil_start.reshape(1, 32), live_count.reshape(1, 32),
        wall_mask, wall_dir, stiffness, start_disp,
    )


def solution(mesh):
    tiles = P(("gx", "gy", "gz"), None)
    flat = P(("gx", "gy", "gz"))
    in_specs = (tiles,) * 7 + (flat, flat, P("gx", "gy"), P(None, "gx", "gy"), P("gx", "gy", "gz"), P(None, "gx", "gy", "gz"))
    out_specs = (tiles, P(None, "gx", "gy", "gz"))
    return jax.shard_map(local, mesh=mesh, in_specs=in_specs, out_specs=out_specs, check_vma=False)
```

time: 587 us -> 49 us (0.08); the launches traced: 575 us -> 48.8 us
  other arithmetic: 308 us -> 0 us
  local copies, waits for them, and re-layouts: 111 us -> 3.99 us
  starting transfers between devices: 101 us -> 0 us
  Pallas kernels: 0 us -> 44.2 us
  waiting for transfers between devices: 30.9 us -> 0 us
  blocking collectives: 22.5 us -> 0 us
    scatter-add x4 -> x0, other arithmetic: 228 us -> none  [the longest x1 57 us: deposit(): jax.ops.segment_sum(terms[:, 0].reshape(-1), first, num_segments=segments)]
    ppermute x30 -> x0, starting transfers between devices: 90.8 us -> none  [the longest x15 67.7 us: extended(): lax.ppermute(lax.slice_in_dim(block, block.shape[dim] - width, None, axis...]
    pallas_call x0 -> x1, Pallas kernels: none -> 44.2 us  [local(): pl.pallas_call(kernel, out_shape=(jax.ShapeDtypeStruct(back_temp.shape, F...]
    div x5 -> x0, other arithmetic: 39.4 us -> none  [the longest x4 39.4 us: relax(): return total / weight]
    scatter-add x4 -> x0, local copies, waits for them, and re-layouts: 36.7 us -> none  [local(): padded = padded.at[:, 1:-1, 1:-1, 0].add(ghost)]
    concatenate x10 -> x0, other arithmetic: 31.3 us -> none  [the longest x9 30.6 us: extended(): block = jnp.concatenate([low, block, high], axis=dim)]
    ppermute x30 -> x0, waiting for transfers between devices: 30.9 us -> none  [the longest x15 29.7 us: extended(): lax.ppermute(lax.slice_in_dim(block, 0, width, axis=dim), axis, backward)]
    psum x1 -> x0, blocking collectives: 22.5 us -> none  [local(): summed = lax.psum(jnp.stack([local_numer, local_denom], axis=0), 'gz')]
  transfers between devices with their start and end apart: 32 -> 0, of which waited for: 12 -> 0; matrix products, arithmetic and copies ran while one was open for 47% -> 0% of each run, Pallas kernels for 0% -> 0%
where the time goes in v1:
time: 49 us; the launch traced here: 48.8 us
  Pallas kernels  44.2 us (90%)
  local copies, waits for them, and re-layouts  3.99 us (8%)
  between operations  0.64 us (1%)
    pallas_call x1, Pallas kernels, local(): pl.pallas_call(kernel, out_shape=(jax.ShapeDtypeStruct(back_temp.shape, F...  44.2 us
    unnamed x2, local copies, waits for them, and re-layouts  3.99 us

profile of v1, /device:TPU:1, one launch (start us, length us, event | category | flops | bytes accessed | tf_op | source)
XLA Modules:
  0.0 48.8 jit_solution(3407193717628542592)
XLA Ops:
  0.6 44.2 %shard_map.140 = (f32[32,128]{1,0:T(8,128)}, f32[3,32,32,128]{3,2,1,0:T(8,128)}) custom-call(f32[32,128]{1,0:T(8,128)} %recovery_temp.1, f32[32,128]{1,0:T(8,128)} %film_coeff.1, f32[32,128]{1,0:T(8,128)} %emissivity.1, f32[32,128]{1,0:T(8,128)} %char_density.1, f32[32,128]{1,0:T(8,128)} %back_temp.1, f32[32,128]{1,0:T(8,128)} %stencil_frac.1, ...), custom_call_target="tpu_custom_call" | custom-call | tf_op jit(solution)/shard_map/pallas_call | solution.py:591
  44.8 1.3 %copy.17 = f32[32,128]{1,0:T(8,128)} copy(f32[32,128]{1,0:T(8,128)} %get-tuple-element.4) | data formatting | bytes 32768
  46.1 2.7 %copy.18 = f32[3,32,32,128]{3,2,1,0:T(8,128)} copy(f32[3,32,32,128]{3,2,1,0:T(8,128)} %get-tuple-element.5) | data formatting | bytes 3145728

commit v2 on v1

v2 whole, which is shorter than its diff:
```python
import jax
import jax.numpy as jnp
from jax import lax
from jax.experimental import pallas as pl
from jax.experimental.pallas import tpu as pltpu
from jax.sharding import PartitionSpec as P

NEWTON = 6
SWEEPS = 4
MESH = pl.DeviceIdType.MESH
F32 = jnp.float32
SIZES = {"gx": 8, "gy": 4, "gz": 8}
EXT = 40

arrhenius_scale = 0.5
activation = 3.0
blowing = 0.5
heat_release = 0.3
radiation = 0.05
conduction = 0.5
time_step = 1.5


def ablation_rate(surface):
    return arrhenius_scale * jnp.exp(activation * (1.0 - 1.0 / surface))


def balance_step(surface, recovery_temp, film_coeff, emissivity, back_temp):
    ablate = ablation_rate(surface)
    film = film_coeff * film_coeff / (film_coeff + blowing * ablate)
    cubed = surface * surface * surface
    imbalance = (
        film * (recovery_temp - surface)
        + heat_release * ablate
        - radiation * emissivity * (cubed * surface)
        - conduction * (surface - back_temp)
    )
    slope = film + 4.0 * radiation * emissivity * cubed + conduction
    return surface + imbalance / slope


def lanes(shape):
    return lax.broadcasted_iota(jnp.int32, shape, len(shape) - 1)


def rows(shape):
    return lax.broadcasted_iota(jnp.int32, shape, len(shape) - 2)


def spot(x):
    return (x + 4) % 5, (x + 4) // 5


def kernel(
    recovery_temp, film_coeff, emissivity, char_density, back_temp, stencil_frac,
    wall_owner, stencil_start, live_count, wall_mask, wall_dir, stiffness, start_disp,
    surface_out, disp_out,
    recovery_v, film_v, emissivity_v, char_v, back_v, frac_v, owner_v, start_v, live_v, mask_v, dir_v, surface_v,
    planes, strip_up, strip_down, strip_from_below, strip_from_above,
    slab_up, slab_down, slab_below, slab_above, edge_send, edge_recv, cross_send, cross_recv,
    ends, halos, weights, field_a, field_b, result,
    side_weights, side_a, side_b, side_source,
    dep_send, dep_recv, ghost, ghost_cross, ghost_side, ghost_face, ghost_corner, ghost_all,
    local_sem, send_sem, recv_sem, dep_sem,
):
    gx, gy, gz = (lax.axis_index(a) for a in ("gx", "gy", "gz"))
    position = (gx, gy, gz)
    limits = (SIZES["gx"], SIZES["gy"], SIZES["gz"])

    def there(step):
        found = None
        for p, d, n in zip(position, step, limits):
            if d != 0:
                ok = (p + d >= 0) & (p + d < n)
                found = ok if found is None else found & ok
        return found

    def target(step):
        return tuple(p + d for p, d in zip(position, step))

    def back(step):
        return tuple(-d for d in step)

    on_wall = gz == 0

    class Message:
        def __init__(self, channel, step, src, dst, walls=False):
            self.to, self.origin = there(step), there(back(step))
            if walls:
                self.to, self.origin = self.to & on_wall, self.origin & on_wall
            self.copy = pltpu.make_async_remote_copy(
                src_ref=src, dst_ref=dst, send_sem=send_sem.at[channel], recv_sem=recv_sem.at[channel],
                device_id=target(step), device_id_type=MESH,
            )

        def start(self):
            pl.when(self.to)(self.copy.start)

        def wait_recv(self):
            pl.when(self.origin)(self.copy.wait_recv)

        def wait_send(self):
            pl.when(self.to)(self.copy.wait_send)

    small = [
        pltpu.make_async_copy(src, dst, local_sem.at[8 + k])
        for k, (src, dst) in enumerate((
            (recovery_temp, recovery_v), (film_coeff, film_v), (emissivity, emissivity_v), (char_density, char_v),
            (back_temp, back_v), (stencil_frac, frac_v), (wall_owner, owner_v), (stencil_start, start_v),
            (live_count, live_v), (wall_mask, mask_v), (wall_dir, dir_v),
        ))
    ]
    for copy in small:
        copy.start()
    load_u = pltpu.make_async_copy(start_disp, planes.at[0:3, 4:36, 0:32], local_sem.at[0])
    load_k = pltpu.make_async_copy(stiffness, planes.at[3, 4:36, 0:32], local_sem.at[1])
    load_u.start()
    load_k.start()

    barrier = pltpu.get_barrier_semaphore()
    near = [(1, 0, 0), (-1, 0, 0), (0, 1, 0), (0, -1, 0), (0, 0, 1), (0, 0, -1)]
    near += [(0, a, b) for a in (1, -1) for b in (1, -1)]
    corners = [(a, b, 0) for a in (1, -1) for b in (1, -1)]
    expected = jnp.where(on_wall, 3, 4)

    def greet(step, ok):
        pl.when(ok)(lambda: pl.semaphore_signal(barrier, inc=1, device_id=target(step), device_id_type=MESH))
        return ok.astype(jnp.int32)

    for step in near:
        expected = expected + greet(step, there(step))
    for step in corners:
        expected = expected + greet(step, there(step) & on_wall)
    rank = gy * limits[2] + gz
    for y in range(limits[1]):
        for z in range(limits[2]):
            pl.when(on_wall & (rank != y * limits[2] + z))(
                lambda y=y, z=z: pl.semaphore_signal(barrier, inc=1, device_id=(gx, y, z), device_id_type=MESH)
            )

    for copy in small:
        copy.wait()
    back_t = back_v[...]
    surface = back_t
    for _ in range(NEWTON):
        surface = balance_step(surface, recovery_v[...], film_v[...], emissivity_v[...], back_t)
    surface_v[...] = surface
    surface_copy = pltpu.make_async_copy(surface_v, surface_out, local_sem.at[7])
    surface_copy.start()
    recession = time_step * ablation_rate(surface) / char_v[...]
    shape = (32, 128)
    lane = lanes(shape)
    square = (32, 32)
    diagonal = rows(square) == lanes(square)

    def column(row):
        spread = jnp.broadcast_to(row.astype(F32), square)
        return jnp.broadcast_to(jnp.sum(jnp.where(diagonal, spread, 0.0), axis=1, keepdims=True), shape)

    starts = start_v[...]
    shift = column(starts & 127)
    live = lane.astype(F32) < column(live_v[...])
    upper = jnp.where(live, frac_v[...], 0.0)
    lower = jnp.where(live, 1.0 - frac_v[...], 0.0)
    shift = shift.astype(jnp.int32)
    first, second = [], []
    for low, high in ((lower * recession, upper * recession), (lower, upper)):
        moved = pltpu.roll(high, 1, axis=1)
        spread = low + jnp.where(lane >= 1, moved, 0.0)
        last = jnp.broadcast_to(moved[:, 0:1], shape)
        for bit in range(7):
            spread = jnp.where(((shift >> bit) & 1) == 1, pltpu.roll(spread, 1 << bit, axis=1), spread)
        first.append(jnp.where(lane >= shift, spread, 0.0))
        second.append(jnp.where(lane < shift, spread, jnp.where(lane == shift, last, 0.0)))
    face_row = owner_v[...] * 8
    row_a = jnp.broadcast_to(face_row + (starts >> 7), square)
    row_b = jnp.broadcast_to(face_row + (((starts >> 7) + 1) & 7), square)

    def gathered(row, terms):
        pick = (rows(square) == row).astype(F32)
        return jnp.dot(pick, terms, precision=lax.Precision.HIGHEST, preferred_element_type=F32)

    summed = gathered(row_a, jnp.concatenate(first, axis=1)) + gathered(row_b, jnp.concatenate(second, axis=1))
    for o in range(4):
        dep_send[o, 0:8] = summed[8 * o : 8 * o + 8, 0:128]
        dep_send[o, 8:16] = summed[8 * o : 8 * o + 8, 128:256]

    tile = (8, 128)
    top = rows(tile) < 4
    tile_lane = lanes(tile)
    load_u.wait()
    load_k.wait()

    def group(lane):
        return ((lane + 4) & 127) // 16

    def pack_ends(c, x_list, first, count, keep):
        size = (count, 128)
        where = group(lanes(size))
        for i in range(5):
            found = [x for x in x_list if spot(x)[0] == i]
            packed = ends[c, i, first : first + count] if keep else jnp.zeros(size, F32)
            for x in found:
                turned = pltpu.roll(planes[c, x + 4, first : first + count], 16 * spot(x)[1] + 4, axis=1)
                packed = jnp.where(where == spot(x)[1], turned, packed)
            if found or not keep:
                ends[c, i, first : first + count] = packed

    inside = range(32)
    outside = (-4, -3, -2, -1, 32, 33, 34, 35)

    def pack_own(c, _):
        pack_ends(c, inside, 0, 32, False)
        return 0

    lax.fori_loop(0, 4, pack_own, 0)
    quarter = lanes(shape) % 16 // 4
    for i in range(5):
        up, down = jnp.zeros(shape, F32), jnp.zeros(shape, F32)
        for c in range(4):
            both = ends[c, i, 0:32]
            up = jnp.where(quarter == c, pltpu.roll(both, 4 * c, axis=1) if c else both, up)
            down = jnp.where(quarter == c, pltpu.roll(both, (4 * c - 4) % 128, axis=1) if c != 1 else both, down)
        slab_up[i] = up
        slab_down[i] = down

    def rows_down(a, b):
        return jnp.where(top, a, pltpu.roll(b, 4, axis=0))

    def rows_up(a, b):
        return jnp.where(top, pltpu.roll(b, 4, axis=0), a)

    def pack_y(x, _):
        for pair in range(2):
            a, b = 2 * pair, 2 * pair + 1
            strip_down[pair, x] = rows_down(planes[a, x + 4, 0:8], planes[b, x + 4, 0:8])
            strip_up[pair, x] = rows_up(planes[a, x + 4, 24:32], planes[b, x + 4, 24:32])
        return 0

    lax.fori_loop(0, 32, pack_y, 0)
    for pair in range(3):
        a, b = 2 * pair, min(2 * pair + 1, 4)
        edge_send[0, pair] = rows_down(slab_up[a, 0:8], slab_up[b, 0:8])
        edge_send[1, pair] = rows_up(slab_up[a, 24:32], slab_up[b, 24:32])
        edge_send[2, pair] = rows_down(slab_down[a, 0:8], slab_down[b, 0:8])
        edge_send[3, pair] = rows_up(slab_down[a, 24:32], slab_down[b, 24:32])

    east, west, north, south = (1, 0, 0), (-1, 0, 0), (0, 1, 0), (0, -1, 0)
    x_far = [
        Message(0, east, start_disp.at[:, 28:32], planes.at[0:3, 0:4, 0:32]),
        Message(1, east, stiffness.at[28:32], planes.at[3, 0:4, 0:32]),
        Message(2, west, start_disp.at[:, 0:4], planes.at[0:3, 36:40, 0:32]),
        Message(3, west, stiffness.at[0:4], planes.at[3, 36:40, 0:32]),
    ]
    y_far = [Message(4, north, strip_up, strip_from_below), Message(5, south, strip_down, strip_from_above)]
    z_far = [
        Message(6, (0, 0, 1), slab_up, slab_below.at[:, 0:32]),
        Message(7, (0, 0, -1), slab_down, slab_above.at[:, 0:32]),
    ]
    edges = [
        Message(8, (0, -1, 1), edge_send.at[0], edge_recv.at[0]),
        Message(9, (0, 1, 1), edge_send.at[1], edge_recv.at[1]),
        Message(10, (0, -1, -1), edge_send.at[2], edge_recv.at[2]),
        Message(11, (0, 1, -1), edge_send.at[3], edge_recv.at[3]),
    ]

    pl.semaphore_wait(barrier, expected)

    def deposit_copy(y):
        ahead = lax.rem(rank - y * limits[2] + 32, 32)
        slot = jnp.maximum(ahead - 1, 0)
        copy = pltpu.make_async_remote_copy(
            src_ref=dep_send.at[y], dst_ref=dep_recv.at[slot], send_sem=send_sem.at[24 + y], recv_sem=dep_sem.at[0],
            device_id=(gx, y, 0), device_id_type=MESH,
        )
        return ahead != 0, copy

    for message in y_far + z_far + edges:
        message.start()
    for y in range(4):
        away, copy = deposit_copy(y)
        pl.when(away)(copy.start)
    for message in x_far:
        message.start()

    def clear(step, *refs):
        @pl.when(jnp.logical_not(there(step)))
        def _():
            for ref in refs:
                ref[...] = jnp.zeros(ref.shape, F32)

    clear(north, strip_from_above)
    clear(south, strip_from_below)
    clear((0, 0, -1), slab_below.at[:, 0:32])
    clear((0, 0, 1), slab_above.at[:, 0:32])
    for k, message_step in enumerate(((0, -1, 1), (0, 1, 1), (0, -1, -1), (0, 1, -1))):
        clear(back(message_step), edge_recv.at[k])
    clear(west, planes.at[:, 0:4, 0:32], planes.at[:, 1:4, 32:40], cross_recv.at[0])
    clear(east, planes.at[:, 36:40, 0:32], planes.at[:, 36:39, 32:40], cross_recv.at[1])
    planes[:, 0, 32:40] = jnp.zeros((4, 8, 128), F32)
    planes[:, 39, 32:40] = jnp.zeros((4, 8, 128), F32)

    for message in y_far:
        message.wait_recv()

    def merged(from_above, from_below):
        a = jnp.where(top, from_above, from_below)
        b = pltpu.roll(jnp.where(top, from_below, from_above), 4, axis=0)
        return a, b

    def merge_y(x, _):
        for pair in range(2):
            a, b = merged(strip_from_above[pair, x], strip_from_below[pair, x])
            planes[2 * pair, x + 4, 32:40] = a
            planes[2 * pair + 1, x + 4, 32:40] = b
        return 0

    lax.fori_loop(0, 32, merge_y, 0)
    x_rows = [
        Message(12, east, planes.at[:, 33:36, 32:40], planes.at[:, 1:4, 32:40]),
        Message(13, west, planes.at[:, 4:7, 32:40], planes.at[:, 36:39, 32:40]),
    ]
    for message in x_rows:
        message.start()

    for message in z_far + edges:
        message.wait_recv()
    for pair in range(3):
        a, b = merged(edge_recv[0, pair], edge_recv[1, pair])
        slab_below[2 * pair, 32:40] = a
        if pair < 2:
            slab_below[2 * pair + 1, 32:40] = b
        a, b = merged(edge_recv[2, pair], edge_recv[3, pair])
        slab_above[2 * pair, 32:40] = a
        if pair < 2:
            slab_above[2 * pair + 1, 32:40] = b
    tall = (EXT, 128)
    sixteen = lanes(tall) // 16
    far_x = ((28, 29, 30, 31), (0, 1, 2, 3))
    halo_x = ((-4, -3, -2, -1), (32, 33, 34, 35))
    for d in range(2):
        cross = jnp.zeros(tall, F32)
        for k, x in enumerate(far_x[d]):
            i, g = spot(x)
            cross = jnp.where(sixteen == k, pltpu.roll(slab_below[i], (16 * (k - g)) % 128, axis=1), cross)
            cross = jnp.where(sixteen == 4 + k, pltpu.roll(slab_above[i], (16 * (4 + k - g)) % 128, axis=1), cross)
        cross_send[d] = cross
    x_cross = [
        Message(14, east, cross_send.at[0], cross_recv.at[0]),
        Message(15, west, cross_send.at[1], cross_recv.at[1]),
    ]
    for message in x_cross:
        message.start()

    def spread(c, X, j):
        return planes[c, X, pl.ds(j, 8, stride=5), :]

    def beside_y(read, c, X, j):
        above = read(c, X, j + 1) if j < 4 else pltpu.roll(read(c, X, 0), 7, axis=0)
        below = read(c, X, j - 1) if j > 0 else pltpu.roll(read(c, X, 4), 1, axis=0)
        return above, below

    def weigh(X):
        for j in range(5):
            centre = spread(3, X, j)
            above, below = beside_y(spread, 3, X, j)
            sides = (
                spread(3, X + 1, j), spread(3, X - 1, j), above, below,
                pltpu.roll(centre, 127, axis=1), pltpu.roll(centre, 1, axis=1),
            )
            weight = 6.0 * centre
            for side in sides:
                weight = weight + side
            inverse = jnp.where(centre > 0.0, 1.0 / weight, 0.0)
            for n, side in enumerate(sides):
                weights[n, X, j] = (centre + side) * inverse

    def reader(field):
        return lambda c, X, j: field[c, X, j]

    def to_field(field):
        def write(c, X, j, value):
            field[c, X, j] = value

        return write

    def to_result(c, X, j, value):
        result[c, X - 4, pl.ds(j, 8, stride=5), :] = value

    def relax(read, write, X):
        for j in range(5):
            w = [weights[n, X, j] for n in range(6)]
            for c in range(3):
                centre = read(c, X, j)
                above, below = beside_y(read, c, X, j)
                total = w[0] * read(c, X + 1, j) + w[1] * read(c, X - 1, j)
                total = total + (w[2] * above + w[3] * below)
                total = total + (w[4] * pltpu.roll(centre, 127, axis=1) + w[5] * pltpu.roll(centre, 1, axis=1))
                write(c, X, j, total)

    def span(body, start, stop, many):
        def step(k, _):
            first = jnp.minimum(start + k * many, stop - many)
            for n in range(many):
                body(first + n)
            return 0

        lax.fori_loop(0, -(-(stop - start) // many), step, 0)

    stages = (
        (spread, to_field(field_a)), (reader(field_a), to_field(field_b)),
        (reader(field_b), to_field(field_a)), (reader(field_a), to_result),
    )
    MANY = 4
    span(weigh, 5, 35, 2)
    for sweep, (read, write) in enumerate(stages):
        span(lambda X, read=read, write=write: relax(read, write, X), 5 + sweep, 35 - sweep, MANY)

    @pl.when(on_wall)
    def _():
        everyone = pltpu.make_async_remote_copy(
            src_ref=dep_recv, dst_ref=dep_recv, send_sem=send_sem.at[24], recv_sem=dep_sem.at[0],
            device_id=(gx, 0, 0), device_id_type=MESH,
        )
        everyone.wait_recv()
        total = dep_send[gy]
        for k in range(31):
            total = total + dep_recv[k]
        face = total[0:8] / (1.0 + total[8:16])
        wide = (8, 640)
        at = lanes(wide)
        which = 5 * (at % 128 // 16) + at // 128 - 4
        acc = jnp.zeros((96, 640), F32)
        for q in range(4):
            mask = mask_v[pl.ds(q, 8, stride=4), :].astype(F32)
            part = face[:, 32 * q : 32 * q + 32] * (-mask)
            values = jnp.concatenate([part * dir_v[c, pl.ds(q, 8, stride=4), :] for c in range(3)], axis=1)
            pick = ((at % 16 == 3) & (which == 4 * rows(wide) + q)).astype(F32)
            acc = acc + lax.dot_general(
                values, pick, (((0,), (0,)), ((), ())), precision=lax.Precision.HIGHEST, preferred_element_type=F32
            )
        short = (32, 128)
        eighth = lanes(short) // 16
        for c in range(3):
            own = [acc[32 * c : 32 * c + 32, 128 * i : 128 * i + 128] for i in range(5)]
            for i in range(5):
                ghost[i, c] = own[i]
            for d in range(2):
                cross = jnp.zeros(short, F32)
                for k, x in enumerate(far_x[d]):
                    i, g = spot(x)
                    cross = jnp.where(eighth == k, pltpu.roll(own[i], (16 * (k - g)) % 128, axis=1), cross)
                ghost_cross[d, c] = cross

    g_side = [
        Message(16, north, ghost.at[:, :, 24:32], ghost_side.at[0], True),
        Message(17, south, ghost.at[:, :, 0:8], ghost_side.at[1], True),
    ]
    g_face = [
        Message(18, east, ghost_cross.at[0], ghost_face.at[0], True),
        Message(19, west, ghost_cross.at[1], ghost_face.at[1], True),
    ]
    g_corner = [
        Message(20, (1, 1, 0), ghost_cross.at[0, :, 24:32], ghost_corner.at[0], True),
        Message(21, (1, -1, 0), ghost_cross.at[0, :, 0:8], ghost_corner.at[1], True),
        Message(22, (-1, 1, 0), ghost_cross.at[1, :, 24:32], ghost_corner.at[2], True),
        Message(23, (-1, -1, 0), ghost_cross.at[1, :, 0:8], ghost_corner.at[3], True),
    ]
    g_all = g_side + g_face + g_corner
    for message in g_all:
        message.start()
    clear(south, ghost_side.at[0])
    clear(north, ghost_side.at[1])
    clear(west, ghost_face.at[0])
    clear(east, ghost_face.at[1])
    for k, step in enumerate(((1, 1, 0), (1, -1, 0), (-1, 1, 0), (-1, -1, 0))):
        clear(back(step), ghost_corner.at[k])

    for message in x_far + x_rows:
        message.wait_recv()
    span(weigh, 1, 5, 2)
    span(weigh, 35, 39, 2)
    for sweep, (read, write) in enumerate(stages):
        span(lambda X, read=read, write=write: relax(read, write, X), 1 + sweep, 5 + sweep, 4)
        span(lambda X, read=read, write=write: relax(read, write, X), 35 - sweep, 39 - sweep, 4)

    for message in x_cross:
        message.wait_recv()

    def pack_rest(c, _):
        pack_ends(c, inside, 32, 8, False)
        pack_ends(c, outside, 0, 32, True)
        pack_ends(c, outside, 32, 8, True)
        return 0

    lax.fori_loop(0, 4, pack_rest, 0)
    for d in range(2):
        for k, x in enumerate(halo_x[d]):
            i, g = spot(x)
            from_below = pltpu.roll(cross_recv[d], (16 * (g - k)) % 128, axis=1)
            from_above = pltpu.roll(cross_recv[d], (16 * (g - 4 - k)) % 128, axis=1)
            slab_below[i] = jnp.where(sixteen == g, from_below, slab_below[i])
            slab_above[i] = jnp.where(sixteen == g, from_above, slab_above[i])
    place = lanes(tall) % 16
    for c in range(4):
        for i in range(5):
            under = pltpu.roll(slab_below[i], (128 - 4 * c) % 128, axis=1) if c else slab_below[i]
            over = pltpu.roll(slab_above[i], (4 - 4 * c) % 128, axis=1) if c != 1 else slab_above[i]
            halos[c, i] = jnp.where(place < 4, under, jnp.where(place < 8, over, 0.0))

    side_source[...] = jnp.zeros(side_source.shape, F32)

    @pl.when(on_wall)
    def _():
        for message in g_all:
            message.wait_recv()
        eighth = lanes((32, 128)) // 16
        eighth_tile = tile_lane // 16
        for c in range(3):
            whole = [ghost[i, c] for i in range(5)]
            rest = [jnp.where(top, ghost_side[1, i, c], ghost_side[0, i, c]) for i in range(5)]
            for d in range(2):
                face = ghost_face[d, c]
                corner = jnp.where(top, ghost_corner[2 * d + 1, c], ghost_corner[2 * d, c])
                for k, x in enumerate(halo_x[d]):
                    i, g = spot(x)
                    whole[i] = jnp.where(eighth == g, pltpu.roll(face, (16 * (g - k)) % 128, axis=1), whole[i])
                    rest[i] = jnp.where(eighth_tile == g, pltpu.roll(corner, (16 * (g - k)) % 128, axis=1), rest[i])
            for i in range(5):
                ghost_all[c, i, 0:32] = whole[i]
                ghost_all[c, i, 32:40] = rest[i]
        for c in range(3):
            for i in range(5):
                for j in range(5):
                    side_source[c, i, j] = ghost_all[c, i, pl.ds(j, 8, stride=5), :]

    tile_place = tile_lane % 16
    low_end = (tile_place >= 4) & (tile_place < 12)
    high_end = (tile_place >= 12) | (tile_place < 4)

    def side_raw(step, _):
        c, i = lax.div(step, 5), lax.rem(step, 5)
        for j in range(5):
            own = ends[c, i, pl.ds(j, 8, stride=5), :]
            halo = halos[c, i, pl.ds(j, 8, stride=5), :]
            low = jnp.where(low_end, own, halo)
            side_a[0, c, i, j] = low
            side_a[1, c, i, j] = jnp.where(high_end, own, halo)
        return 0

    lax.fori_loop(0, 20, side_raw, 0)
    for c in range(3):
        for i in range(5):
            for j in range(5):
                side_a[0, c, i, j] = side_a[0, c, i, j] + side_source[c, i, j]

    def side_sides(field, e, c, i, j):
        here = field[e, c, i, j]
        return (
            field[e, c, i + 1, j] if i < 4 else pltpu.roll(field[e, c, 0, j], 112, axis=1),
            field[e, c, i - 1, j] if i > 0 else pltpu.roll(field[e, c, 4, j], 16, axis=1),
            field[e, c, i, j + 1] if j < 4 else pltpu.roll(field[e, c, i, 0], 7, axis=0),
            field[e, c, i, j - 1] if j > 0 else pltpu.roll(field[e, c, i, 4], 1, axis=0),
            pltpu.roll(here, 127, axis=1),
            pltpu.roll(here, 1, axis=1),
        )

    def side_weigh(e, _):
        for i in range(5):
            for j in range(5):
                centre = side_a[e, 3, i, j]
                sides = side_sides(side_a, e, 3, i, j)
                weight = 6.0 * centre
                for side in sides:
                    weight = weight + side
                inverse = jnp.where(centre > 0.0, 1.0 / weight, 0.0)
                for n, side in enumerate(sides):
                    side_weights[n, e, i, j] = (centre + side) * inverse
        return 0

    lax.fori_loop(0, 2, side_weigh, 0)
    for sweep in range(SWEEPS):
        src, dst = (side_a, side_b) if sweep % 2 == 0 else (side_b, side_a)
        for e in range(2):

            def side_relax(c, _, src=src, dst=dst, e=e):
                for i in range(5):
                    for j in range(5):
                        sides = side_sides(src, e, c, i, j)
                        total = side_weights[0, e, i, j] * sides[0]
                        for n in range(1, 6):
                            total = total + side_weights[n, e, i, j] * sides[n]
                        dst[e, c, i, j] = total + side_source[c, i, j] if e == 0 else total
                return 0

            lax.fori_loop(0, 3, side_relax, 0)

    edge_lane = (tile_lane < 4) | (tile_lane >= 124)
    outs = []
    for c in range(3):

        def put_back(j, _, c=c):
            for i in range(5):
                both = jnp.where(tile_place < 4, side_a[1, c, i, j], side_a[0, c, i, j])
                for x in inside:
                    if spot(x)[0] == i:
                        turned = pltpu.roll(both, 128 - 16 * spot(x)[1] - 4, axis=1)
                        here = pl.ds(j, 8, stride=5)
                        result[c, x, here, :] = jnp.where(edge_lane, turned, result[c, x, here, :])
            return 0

        lax.fori_loop(0, 5, put_back, 0)
        copy = pltpu.make_async_copy(result.at[c, :, 0:32], disp_out.at[c], local_sem.at[2 + c])
        copy.start()
        outs.append(copy)

    for message in x_far + y_far + z_far + edges + x_rows + x_cross + g_all:
        message.wait_send()
    for y in range(4):
        away, copy = deposit_copy(y)
        pl.when(away)(copy.wait_send)
    for copy in outs:
        copy.wait()
    surface_copy.wait()


def local(
    recovery_temp, film_coeff, emissivity, char_density, back_temp, stencil_frac,
    wall_owner, stencil_start, live_count, wall_mask, wall_dir, stiffness, start_disp,
):
    hbm = pl.BlockSpec(memory_space=pl.ANY)
    def f32(*shape):
        return pltpu.VMEM(shape, F32)

    def i32(*shape):
        return pltpu.VMEM(shape, jnp.int32)

    scratch = [f32(32, 128)] * 6 + [i32(1, 32)] * 3 + [i32(32, 32), f32(3, 32, 32), f32(32, 128)]
    scratch += [
        f32(4, EXT, EXT, 128),
        f32(2, 32, 8, 128),
        f32(2, 32, 8, 128),
        f32(2, 32, 8, 128),
        f32(2, 32, 8, 128),
        f32(5, 32, 128),
        f32(5, 32, 128),
        f32(5, EXT, 128),
        f32(5, EXT, 128),
        f32(4, 3, 8, 128),
        f32(4, 3, 8, 128),
        f32(2, EXT, 128),
        f32(2, EXT, 128),
        f32(4, 5, EXT, 128),
        f32(4, 5, EXT, 128),
        f32(6, EXT, 5, 8, 128),
        f32(3, EXT, 5, 8, 128),
        f32(3, EXT, 5, 8, 128),
        f32(3, 32, EXT, 128),
        f32(6, 2, 5, 5, 8, 128),
        f32(2, 4, 5, 5, 8, 128),
        f32(2, 3, 5, 5, 8, 128),
        f32(3, 5, 5, 8, 128),
        f32(4, 16, 128),
        f32(31, 16, 128),
        f32(5, 3, 32, 128),
        f32(2, 3, 32, 128),
        f32(2, 5, 3, 8, 128),
        f32(2, 3, 32, 128),
        f32(4, 3, 8, 128),
        f32(3, 5, EXT, 128),
    ]
    return pl.pallas_call(
        kernel,
        out_shape=(
            jax.ShapeDtypeStruct(back_temp.shape, F32),
            jax.ShapeDtypeStruct(start_disp.shape, F32),
        ),
        in_specs=[hbm] * 13,
        out_specs=(hbm, hbm),
        scratch_shapes=scratch
        + [
            pltpu.SemaphoreType.DMA((19,)),
            pltpu.SemaphoreType.DMA((28,)),
            pltpu.SemaphoreType.DMA((24,)),
            pltpu.SemaphoreType.DMA((1,)),
        ],
        compiler_params=pltpu.CompilerParams(collective_id=0, has_side_effects=True, vmem_limit_bytes=60 << 20),
    )(
        recovery_temp, film_coeff, emissivity, char_density, back_temp, stencil_frac,
        wall_owner.reshape(1, 32), stencil_start.reshape(1, 32), live_count.reshape(1, 32),
        wall_mask, wall_dir, stiffness, start_disp,
    )


def solution(mesh):
    tiles = P(("gx", "gy", "gz"), None)
    flat = P(("gx", "gy", "gz"))
    in_specs = (tiles,) * 7 + (flat, flat, P("gx", "gy"), P(None, "gx", "gy"), P("gx", "gy", "gz"), P(None, "gx", "gy", "gz"))
    out_specs = (tiles, P(None, "gx", "gy", "gz"))
    return jax.shard_map(local, mesh=mesh, in_specs=in_specs, out_specs=out_specs, check_vma=False)
```

time: 49 us -> 40.1 us (0.82); the launches traced: 48.8 us -> 39.4 us
  Pallas kernels: 44.2 us -> 34.8 us
    pallas_call x1, Pallas kernels: 44.2 us -> 34.8 us  [local(): pl.pallas_call(kernel, out_shape=(jax.ShapeDtypeStruct(back_temp.shape, F...]
where the time goes in v2:
time: 40.1 us; the launch traced here: 39.4 us
  Pallas kernels  34.8 us (87%)
  local copies, waits for them, and re-layouts  3.99 us (10%)
  between operations  0.64 us (2%)
    pallas_call x1, Pallas kernels, local(): pl.pallas_call(kernel, out_shape=(jax.ShapeDtypeStruct(back_temp.shape, F...  34.8 us
    unnamed x2, local copies, waits for them, and re-layouts  3.99 us

profile of v2, /device:TPU:1, one launch (start us, length us, event | category | flops | bytes accessed | tf_op | source)
XLA Modules:
  0.0 39.4 jit_solution(1810013943771612888)
XLA Ops:
  0.6 34.8 %shard_map.140 = (f32[32,128]{1,0:T(8,128)}, f32[3,32,32,128]{3,2,1,0:T(8,128)}) custom-call(f32[32,128]{1,0:T(8,128)} %recovery_temp.1, f32[32,128]{1,0:T(8,128)} %film_coeff.1, f32[32,128]{1,0:T(8,128)} %emissivity.1, f32[32,128]{1,0:T(8,128)} %char_density.1, f32[32,128]{1,0:T(8,128)} %back_temp.1, f32[32,128]{1,0:T(8,128)} %stencil_frac.1, ...), custom_call_target="tpu_custom_call" | custom-call | tf_op jit(solution)/shard_map/pallas_call | solution.py:672
  35.4 1.3 %copy.17 = f32[32,128]{1,0:T(8,128)} copy(f32[32,128]{1,0:T(8,128)} %get-tuple-element.4) | data formatting | bytes 32768
  36.7 2.7 %copy.18 = f32[3,32,32,128]{3,2,1,0:T(8,128)} copy(f32[3,32,32,128]{3,2,1,0:T(8,128)} %get-tuple-element.5) | data formatting | bytes 3145728

commit v3 on v2

--- a/solution.py
+++ b/solution.py
@@ -55,7 +55,7 @@
     recovery_temp, film_coeff, emissivity, char_density, back_temp, stencil_frac,
     wall_owner, stencil_start, live_count, wall_mask, wall_dir, stiffness, start_disp,
     surface_out, disp_out,
-    recovery_v, film_v, emissivity_v, char_v, back_v, frac_v, owner_v, start_v, live_v, mask_v, dir_v, surface_v,
+    recovery_v, film_v, emissivity_v, char_v, back_v, frac_v, owner_v, start_v, live_v, mask_v, dir_v,
     planes, strip_up, strip_down, strip_from_below, strip_from_above,
     slab_up, slab_down, slab_below, slab_above, edge_send, edge_recv, cross_send, cross_recv,
     ends, halos, weights, field_a, field_b, result,
@@ -138,15 +138,67 @@
                 lambda y=y, z=z: pl.semaphore_signal(barrier, inc=1, device_id=(gx, y, z), device_id_type=MESH)
             )
 
+    tile = (8, 128)
+    top = rows(tile) < 4
+    tile_lane = lanes(tile)
+    load_u.wait()
+    load_k.wait()
+
+    def rows_down(a, b):
+        return jnp.where(top, a, pltpu.roll(b, 4, axis=0))
+
+    def rows_up(a, b):
+        return jnp.where(top, pltpu.roll(b, 4, axis=0), a)
+
+    def pack_y(k, _):
+        for x in (8 * k + n for n in range(8)):
+            for pair in range(2):
+                a, b = 2 * pair, 2 * pair + 1
+                strip_down[pair, x] = rows_down(planes[a, x + 4, 0:8], planes[b, x + 4, 0:8])
+                strip_up[pair, x] = rows_up(planes[a, x + 4, 24:32], planes[b, x + 4, 24:32])
+        return 0
+
+    lax.fori_loop(0, 4, pack_y, 0)
+    east, west, north, south = (1, 0, 0), (-1, 0, 0), (0, 1, 0), (0, -1, 0)
+    x_far = [
+        Message(0, east, start_disp.at[:, 28:32], planes.at[0:3, 0:4, 0:32]),
+        Message(1, east, stiffness.at[28:32], planes.at[3, 0:4, 0:32]),
+        Message(2, west, start_disp.at[:, 0:4], planes.at[0:3, 36:40, 0:32]),
+        Message(3, west, stiffness.at[0:4], planes.at[3, 36:40, 0:32]),
+    ]
+    y_far = [Message(4, north, strip_up, strip_from_below), Message(5, south, strip_down, strip_from_above)]
+    z_far = [
+        Message(6, (0, 0, 1), slab_up, slab_below.at[:, 0:32]),
+        Message(7, (0, 0, -1), slab_down, slab_above.at[:, 0:32]),
+    ]
+    edges = [
+        Message(8, (0, -1, 1), edge_send.at[0], edge_recv.at[0]),
+        Message(9, (0, 1, 1), edge_send.at[1], edge_recv.at[1]),
+        Message(10, (0, -1, -1), edge_send.at[2], edge_recv.at[2]),
+        Message(11, (0, 1, -1), edge_send.at[3], edge_recv.at[3]),
+    ]
+
+    pl.semaphore_wait(barrier, expected)
+
+    def deposit_copy(y):
+        ahead = lax.rem(rank - y * limits[2] + 32, 32)
+        slot = jnp.maximum(ahead - 1, 0)
+        copy = pltpu.make_async_remote_copy(
+            src_ref=dep_send.at[y], dst_ref=dep_recv.at[slot], send_sem=send_sem.at[24 + y], recv_sem=dep_sem.at[0],
+            device_id=(gx, y, 0), device_id_type=MESH,
+        )
+        return ahead != 0, copy
+
+    for message in y_far + x_far:
+        message.start()
+
     for copy in small:
         copy.wait()
     back_t = back_v[...]
     surface = back_t
     for _ in range(NEWTON):
         surface = balance_step(surface, recovery_v[...], film_v[...], emissivity_v[...], back_t)
-    surface_v[...] = surface
-    surface_copy = pltpu.make_async_copy(surface_v, surface_out, local_sem.at[7])
-    surface_copy.start()
+    surface_out[...] = surface
     recession = time_step * ablation_rate(surface) / char_v[...]
     shape = (32, 128)
     lane = lanes(shape)
@@ -185,11 +237,9 @@
         dep_send[o, 0:8] = summed[8 * o : 8 * o + 8, 0:128]
         dep_send[o, 8:16] = summed[8 * o : 8 * o + 8, 128:256]
 
-    tile = (8, 128)
-    top = rows(tile) < 4
-    tile_lane = lanes(tile)
-    load_u.wait()
-    load_k.wait()
+    for y in range(4):
+        away, copy = deposit_copy(y)
+        pl.when(away)(copy.start)
 
     def group(lane):
         return ((lane + 4) & 127) // 16
@@ -224,20 +274,6 @@
         slab_up[i] = up
         slab_down[i] = down
 
-    def rows_down(a, b):
-        return jnp.where(top, a, pltpu.roll(b, 4, axis=0))
-
-    def rows_up(a, b):
-        return jnp.where(top, pltpu.roll(b, 4, axis=0), a)
-
-    def pack_y(x, _):
-        for pair in range(2):
-            a, b = 2 * pair, 2 * pair + 1
-            strip_down[pair, x] = rows_down(planes[a, x + 4, 0:8], planes[b, x + 4, 0:8])
-            strip_up[pair, x] = rows_up(planes[a, x + 4, 24:32], planes[b, x + 4, 24:32])
-        return 0
-
-    lax.fori_loop(0, 32, pack_y, 0)
     for pair in range(3):
         a, b = 2 * pair, min(2 * pair + 1, 4)
         edge_send[0, pair] = rows_down(slab_up[a, 0:8], slab_up[b, 0:8])
@@ -245,42 +281,7 @@
         edge_send[2, pair] = rows_down(slab_down[a, 0:8], slab_down[b, 0:8])
         edge_send[3, pair] = rows_up(slab_down[a, 24:32], slab_down[b, 24:32])
 
-    east, west, north, south = (1, 0, 0), (-1, 0, 0), (0, 1, 0), (0, -1, 0)
-    x_far = [
-        Message(0, east, start_disp.at[:, 28:32], planes.at[0:3, 0:4, 0:32]),
-        Message(1, east, stiffness.at[28:32], planes.at[3, 0:4, 0:32]),
-        Message(2, west, start_disp.at[:, 0:4], planes.at[0:3, 36:40, 0:32]),
-        Message(3, west, stiffness.at[0:4], planes.at[3, 36:40, 0:32]),
-    ]
-    y_far = [Message(4, north, strip_up, strip_from_below), Message(5, south, strip_down, strip_from_above)]
-    z_far = [
-        Message(6, (0, 0, 1), slab_up, slab_below.at[:, 0:32]),
-        Message(7, (0, 0, -1), slab_down, slab_above.at[:, 0:32]),
-    ]
-    edges = [
-        Message(8, (0, -1, 1), edge_send.at[0], edge_recv.at[0]),
-        Message(9, (0, 1, 1), edge_send.at[1], edge_recv.at[1]),
-        Message(10, (0, -1, -1), edge_send.at[2], edge_recv.at[2]),
-        Message(11, (0, 1, -1), edge_send.at[3], edge_recv.at[3]),
-    ]
-
-    pl.semaphore_wait(barrier, expected)
-
-    def deposit_copy(y):
-        ahead = lax.rem(rank - y * limits[2] + 32, 32)
-        slot = jnp.maximum(ahead - 1, 0)
-        copy = pltpu.make_async_remote_copy(
-            src_ref=dep_send.at[y], dst_ref=dep_recv.at[slot], send_sem=send_sem.at[24 + y], recv_sem=dep_sem.at[0],
-            device_id=(gx, y, 0), device_id_type=MESH,
-        )
-        return ahead != 0, copy
-
-    for message in y_far + z_far + edges:
-        message.start()
-    for y in range(4):
-        away, copy = deposit_copy(y)
-        pl.when(away)(copy.start)
-    for message in x_far:
+    for message in edges + z_far:
         message.start()
 
     def clear(step, *refs):
@@ -308,20 +309,88 @@
         b = pltpu.roll(jnp.where(top, from_below, from_above), 4, axis=0)
         return a, b
 
-    def merge_y(x, _):
-        for pair in range(2):
-            a, b = merged(strip_from_above[pair, x], strip_from_below[pair, x])
-            planes[2 * pair, x + 4, 32:40] = a
-            planes[2 * pair + 1, x + 4, 32:40] = b
+    def merge_y(k, _):
+        for x in (8 * k + n for n in range(8)):
+            for pair in range(2):
+                a, b = merged(strip_from_above[pair, x], strip_from_below[pair, x])
+                planes[2 * pair, x + 4, 32:40] = a
+                planes[2 * pair + 1, x + 4, 32:40] = b
         return 0
 
-    lax.fori_loop(0, 32, merge_y, 0)
+    lax.fori_loop(0, 4, merge_y, 0)
     x_rows = [
         Message(12, east, planes.at[:, 33:36, 32:40], planes.at[:, 1:4, 32:40]),
         Message(13, west, planes.at[:, 4:7, 32:40], planes.at[:, 36:39, 32:40]),
     ]
     for message in x_rows:
         message.start()
+
+    def spread(c, X, j):
+        return planes[c, X, pl.ds(j, 8, stride=5), :]
+
+    def beside_y(read, c, X, j):
+        above = read(c, X, j + 1) if j < 4 else pltpu.roll(read(c, X, 0), 7, axis=0)
+        below = read(c, X, j - 1) if j > 0 else pltpu.roll(read(c, X, 4), 1, axis=0)
+        return above, below
+
+    def weigh(X):
+        for j in range(5):
+            centre = spread(3, X, j)
+            above, below = beside_y(spread, 3, X, j)
+            sides = (
+                spread(3, X + 1, j), spread(3, X - 1, j), above, below,
+                pltpu.roll(centre, 127, axis=1), pltpu.roll(centre, 1, axis=1),
+            )
+            weight = 6.0 * centre
+            for side in sides:
+                weight = weight + side
+            inverse = jnp.where(centre > 0.0, 1.0 / weight, 0.0)
+            for n, side in enumerate(sides):
+                weights[n, X, j] = (centre + side) * inverse
+
+    def reader(field):
+        return lambda c, X, j: field[c, X, j]
+
+    def to_field(field):
+        def write(c, X, j, value):
+            field[c, X, j] = value
+
+        return write
+
+    def to_result(c, X, j, value):
+        result[c, X - 4, pl.ds(j, 8, stride=5), :] = value
+
+    def relax(read, write, X):
+        for j in range(5):
+            w = [weights[n, X, j] for n in range(6)]
+            for c in range(3):
+                centre = read(c, X, j)
+                above, below = beside_y(read, c, X, j)
+                total = w[0] * read(c, X + 1, j) + w[1] * read(c, X - 1, j)
+                total = total + (w[2] * above + w[3] * below)
+                total = total + (w[4] * pltpu.roll(centre, 127, axis=1) + w[5] * pltpu.roll(centre, 1, axis=1))
+                write(c, X, j, total)
+
+    def span(body, start, stop, many):
+        def step(k, _):
+            first = jnp.minimum(start + k * many, stop - many)
+            for n in range(many):
+                body(first + n)
+            return 0
+
+        lax.fori_loop(0, -(-(stop - start) // many), step, 0)
+
+    stages = (
+        (spread, to_field(field_a)), (reader(field_a), to_field(field_b)),
+        (reader(field_b), to_field(field_a)), (reader(field_a), to_result),
+    )
+    MANY = (10, 14, 13, 12)
+    span(weigh, 5, 35, 10)
+    def interior(sweep):
+        read, write = stages[sweep]
+        span(lambda X: relax(read, write, X), 5 + sweep, 35 - sweep, MANY[sweep])
+
+    interior(0)
 
     for message in z_far + edges:
         message.wait_recv()
@@ -351,70 +420,6 @@
     ]
     for message in x_cross:
         message.start()
-
-    def spread(c, X, j):
-        return planes[c, X, pl.ds(j, 8, stride=5), :]
-
-    def beside_y(read, c, X, j):
-        above = read(c, X, j + 1) if j < 4 else pltpu.roll(read(c, X, 0), 7, axis=0)
-        below = read(c, X, j - 1) if j > 0 else pltpu.roll(read(c, X, 4), 1, axis=0)
-        return above, below
-
-    def weigh(X):
-        for j in range(5):
-            centre = spread(3, X, j)
-            above, below = beside_y(spread, 3, X, j)
-            sides = (
-                spread(3, X + 1, j), spread(3, X - 1, j), above, below,
-                pltpu.roll(centre, 127, axis=1), pltpu.roll(centre, 1, axis=1),
-            )
-            weight = 6.0 * centre
-            for side in sides:
-                weight = weight + side
-            inverse = jnp.where(centre > 0.0, 1.0 / weight, 0.0)
-            for n, side in enumerate(sides):
-                weights[n, X, j] = (centre + side) * inverse
-
-    def reader(field):
-        return lambda c, X, j: field[c, X, j]
-
-    def to_field(field):
-        def write(c, X, j, value):
-            field[c, X, j] = value
-
-        return write
-
-    def to_result(c, X, j, value):
-        result[c, X - 4, pl.ds(j, 8, stride=5), :] = value
-
-    def relax(read, write, X):
-        for j in range(5):
-            w = [weights[n, X, j] for n in range(6)]
-            for c in range(3):
-                centre = read(c, X, j)
-                above, below = beside_y(read, c, X, j)
-                total = w[0] * read(c, X + 1, j) + w[1] * read(c, X - 1, j)
-                total = total + (w[2] * above + w[3] * below)
-                total = total + (w[4] * pltpu.roll(centre, 127, axis=1) + w[5] * pltpu.roll(centre, 1, axis=1))
-                write(c, X, j, total)
-
-    def span(body, start, stop, many):
-        def step(k, _):
-            first = jnp.minimum(start + k * many, stop - many)
-            for n in range(many):
-                body(first + n)
-            return 0
-
-        lax.fori_loop(0, -(-(stop - start) // many), step, 0)
-
-    stages = (
-        (spread, to_field(field_a)), (reader(field_a), to_field(field_b)),
-        (reader(field_b), to_field(field_a)), (reader(field_a), to_result),
-    )
-    MANY = 4
-    span(weigh, 5, 35, 2)
-    for sweep, (read, write) in enumerate(stages):
-        span(lambda X, read=read, write=write: relax(read, write, X), 5 + sweep, 35 - sweep, MANY)
 
     @pl.when(on_wall)
     def _():
@@ -476,13 +481,24 @@
     for k, step in enumerate(((1, 1, 0), (1, -1, 0), (-1, 1, 0), (-1, -1, 0))):
         clear(back(step), ghost_corner.at[k])
 
+    for sweep in (1, 2, 3):
+        interior(sweep)
+
+
     for message in x_far + x_rows:
         message.wait_recv()
-    span(weigh, 1, 5, 2)
-    span(weigh, 35, 39, 2)
+    def both_ends(body, left, right):
+        def step(k, _):
+            start = jnp.where(k == 0, left, right)
+            for n in range(4):
+                body(start + n)
+            return 0
+
+        lax.fori_loop(0, 2, step, 0)
+
+    both_ends(weigh, 1, 35)
     for sweep, (read, write) in enumerate(stages):
-        span(lambda X, read=read, write=write: relax(read, write, X), 1 + sweep, 5 + sweep, 4)
-        span(lambda X, read=read, write=write: relax(read, write, X), 35 - sweep, 39 - sweep, 4)
+        both_ends(lambda X, read=read, write=write: relax(read, write, X), 1 + sweep, 35 - sweep)
 
     for message in x_cross:
         message.wait_recv()
@@ -507,6 +523,61 @@
             under = pltpu.roll(slab_below[i], (128 - 4 * c) % 128, axis=1) if c else slab_below[i]
             over = pltpu.roll(slab_above[i], (4 - 4 * c) % 128, axis=1) if c != 1 else slab_above[i]
             halos[c, i] = jnp.where(place < 4, under, jnp.where(place < 8, over, 0.0))
+
+    tile_place = tile_lane % 16
+    low_end = (tile_place >= 4) & (tile_place < 12)
+    high_end = (tile_place >= 12) | (tile_place < 4)
+
+    def side_raw(step, _):
+        c, i = lax.div(step, 5), lax.rem(step, 5)
+        for j in range(5):
+            own = ends[c, i, pl.ds(j, 8, stride=5), :]
+            halo = halos[c, i, pl.ds(j, 8, stride=5), :]
+            low = jnp.where(low_end, own, halo)
+            side_a[0, c, i, j] = low
+            side_a[1, c, i, j] = jnp.where(high_end, own, halo)
+        return 0
+
+    lax.fori_loop(0, 20, side_raw, 0)
+    def side_sides(field, e, c, i, j):
+        here = field[e, c, i, j]
+        return (
+            field[e, c, i + 1, j] if i < 4 else pltpu.roll(field[e, c, 0, j], 112, axis=1),
+            field[e, c, i - 1, j] if i > 0 else pltpu.roll(field[e, c, 4, j], 16, axis=1),
+            field[e, c, i, j + 1] if j < 4 else pltpu.roll(field[e, c, i, 0], 7, axis=0),
+            field[e, c, i, j - 1] if j > 0 else pltpu.roll(field[e, c, i, 4], 1, axis=0),
+            pltpu.roll(here, 127, axis=1),
+            pltpu.roll(here, 1, axis=1),
+        )
+
+    def side_weigh(e, _):
+        for i in range(5):
+            for j in range(5):
+                centre = side_a[e, 3, i, j]
+                sides = side_sides(side_a, e, 3, i, j)
+                weight = 6.0 * centre
+                for side in sides:
+                    weight = weight + side
+                inverse = jnp.where(centre > 0.0, 1.0 / weight, 0.0)
+                for n, side in enumerate(sides):
+                    side_weights[n, e, i, j] = (centre + side) * inverse
+        return 0
+
+    lax.fori_loop(0, 2, side_weigh, 0)
+    def side_sweeps(e):
+        for sweep in range(SWEEPS):
+            src, dst = (side_a, side_b) if sweep % 2 == 0 else (side_b, side_a)
+
+            for c in range(3):
+                for i in range(5):
+                    for j in range(5):
+                        sides = side_sides(src, e, c, i, j)
+                        total = side_weights[0, e, i, j] * sides[0]
+                        for n in range(1, 6):
+                            total = total + side_weights[n, e, i, j] * sides[n]
+                        dst[e, c, i, j] = total + side_source[c, i, j] if e == 0 else total
+
+    side_sweeps(1)
 
     side_source[...] = jnp.zeros(side_source.shape, F32)
 
@@ -534,108 +605,49 @@
                 for j in range(5):
                     side_source[c, i, j] = ghost_all[c, i, pl.ds(j, 8, stride=5), :]
 
-    tile_place = tile_lane % 16
-    low_end = (tile_place >= 4) & (tile_place < 12)
-    high_end = (tile_place >= 12) | (tile_place < 4)
-
-    def side_raw(step, _):
-        c, i = lax.div(step, 5), lax.rem(step, 5)
-        for j in range(5):
-            own = ends[c, i, pl.ds(j, 8, stride=5), :]
-            halo = halos[c, i, pl.ds(j, 8, stride=5), :]
-            low = jnp.where(low_end, own, halo)
-            side_a[0, c, i, j] = low
-            side_a[1, c, i, j] = jnp.where(high_end, own, halo)
-        return 0
-
-    lax.fori_loop(0, 20, side_raw, 0)
     for c in range(3):
         for i in range(5):
             for j in range(5):
                 side_a[0, c, i, j] = side_a[0, c, i, j] + side_source[c, i, j]
 
-    def side_sides(field, e, c, i, j):
-        here = field[e, c, i, j]
-        return (
-            field[e, c, i + 1, j] if i < 4 else pltpu.roll(field[e, c, 0, j], 112, axis=1),
-            field[e, c, i - 1, j] if i > 0 else pltpu.roll(field[e, c, 4, j], 16, axis=1),
-            field[e, c, i, j + 1] if j < 4 else pltpu.roll(field[e, c, i, 0], 7, axis=0),
-            field[e, c, i, j - 1] if j > 0 else pltpu.roll(field[e, c, i, 4], 1, axis=0),
-            pltpu.roll(here, 127, axis=1),
-            pltpu.roll(here, 1, axis=1),
-        )
-
-    def side_weigh(e, _):
+    side_sweeps(0)
+
+    for c in range(3):
         for i in range(5):
             for j in range(5):
-                centre = side_a[e, 3, i, j]
-                sides = side_sides(side_a, e, 3, i, j)
-                weight = 6.0 * centre
-                for side in sides:
-                    weight = weight + side
-                inverse = jnp.where(centre > 0.0, 1.0 / weight, 0.0)
-                for n, side in enumerate(sides):
-                    side_weights[n, e, i, j] = (centre + side) * inverse
+                both = jnp.where(tile_place < 4, side_a[1, c, i, j], side_a[0, c, i, j])
+                ends[c, i, pl.ds(j, 8, stride=5), :] = both
+    edge_rows = (lanes(shape) < 4) | (lanes(shape) >= 124)
+
+    def put_back(c, _):
+        for x in inside:
+            i, g = spot(x)
+            turned = pltpu.roll(ends[c, i, 0:32], 128 - 16 * g - 4, axis=1)
+            disp_out[c, x] = jnp.where(edge_rows, turned, result[c, x, 0:32])
         return 0
 
-    lax.fori_loop(0, 2, side_weigh, 0)
-    for sweep in range(SWEEPS):
-        src, dst = (side_a, side_b) if sweep % 2 == 0 else (side_b, side_a)
-        for e in range(2):
-
-            def side_relax(c, _, src=src, dst=dst, e=e):
-                for i in range(5):
-                    for j in range(5):
-                        sides = side_sides(src, e, c, i, j)
-                        total = side_weights[0, e, i, j] * sides[0]
-                        for n in range(1, 6):
-                            total = total + side_weights[n, e, i, j] * sides[n]
-                        dst[e, c, i, j] = total + side_source[c, i, j] if e == 0 else total
-                return 0
-
-            lax.fori_loop(0, 3, side_relax, 0)
-
-    edge_lane = (tile_lane < 4) | (tile_lane >= 124)
-    outs = []
-    for c in range(3):
-
-        def put_back(j, _, c=c):
-            for i in range(5):
-                both = jnp.where(tile_place < 4, side_a[1, c, i, j], side_a[0, c, i, j])
-                for x in inside:
-                    if spot(x)[0] == i:
-                        turned = pltpu.roll(both, 128 - 16 * spot(x)[1] - 4, axis=1)
-                        here = pl.ds(j, 8, stride=5)
-                        result[c, x, here, :] = jnp.where(edge_lane, turned, result[c, x, here, :])
-            return 0
-
-        lax.fori_loop(0, 5, put_back, 0)
-        copy = pltpu.make_async_copy(result.at[c, :, 0:32], disp_out.at[c], local_sem.at[2 + c])
-        copy.start()
-        outs.append(copy)
+    lax.fori_loop(0, 3, put_back, 0)
 
     for message in x_far + y_far + z_far + edges + x_rows + x_cross + g_all:
         message.wait_send()
     for y in range(4):
         away, copy = deposit_copy(y)
         pl.when(away)(copy.wait_send)
-    for copy in outs:
-        copy.wait()
-    surface_copy.wait()
 
 
 def local(
     recovery_temp, film_coeff, emissivity, char_density, back_temp, stencil_frac,
     wall_owner, stencil_start, live_count, wall_mask, wall_dir, stiffness, start_disp,
 ):
-    hbm = pl.BlockSpec(memory_space=pl.ANY)
+    vmem = pl.BlockSpec(memory_space=pltpu.VMEM)
+    hbm = pl.BlockSpec(memory_space=pltpu.HBM)
     def f32(*shape):
         return pltpu.VMEM(shape, F32)
 
     def i32(*shape):
         return pltpu.VMEM(shape, jnp.int32)
 
-    scratch = [f32(32, 128)] * 6 + [i32(1, 32)] * 3 + [i32(32, 32), f32(3, 32, 32), f32(32, 128)]
+    scratch = [f32(32, 128)] * 6 + [i32(1, 32)] * 3 + [i32(32, 32), f32(3, 32, 32)]
     scratch += [
         f32(4, EXT, EXT, 128),
         f32(2, 32, 8, 128),
@@ -671,12 +683,9 @@
     ]
     return pl.pallas_call(
         kernel,
-        out_shape=(
-            jax.ShapeDtypeStruct(back_temp.shape, F32),
-            jax.ShapeDtypeStruct(start_disp.shape, F32),
-        ),
+        out_shape=(pltpu.VMEM(back_temp.shape, F32), pltpu.VMEM(start_disp.shape, F32)),
         in_specs=[hbm] * 13,
-        out_specs=(hbm, hbm),
+        out_specs=(vmem, vmem),
         scratch_shapes=scratch
         + [
             pltpu.SemaphoreType.DMA((19,)),
@@ -684,11 +693,16 @@
             pltpu.SemaphoreType.DMA((24,)),
             pltpu.SemaphoreType.DMA((1,)),
         ],
-        compiler_params=pltpu.CompilerParams(collective_id=0, has_side_effects=True, vmem_limit_bytes=60 << 20),
+        compiler_params=pltpu.CompilerParams(collective_id=0, has_side_effects=True, vmem_limit_bytes=32 << 20),
     )(
-        recovery_temp, film_coeff, emissivity, char_density, back_temp, stencil_frac,
-        wall_owner.reshape(1, 32), stencil_start.reshape(1, 32), live_count.reshape(1, 32),
-        wall_mask, wall_dir, stiffness, start_disp,
+        *(
+            pltpu.with_memory_space_constraint(x, pltpu.HBM)
+            for x in (
+                recovery_temp, film_coeff, emissivity, char_density, back_temp, stencil_frac,
+                wall_owner.reshape(1, 32), stencil_start.reshape(1, 32), live_count.reshape(1, 32),
+                wall_mask, wall_dir, stiffness, start_disp,
+            )
+        )
     )
 
 

time: 40.1 us -> 28.1 us (0.70); the launches traced: 39.4 us -> 27.9 us
  Pallas kernels: 34.8 us -> 25.5 us
  local copies, waits for them, and re-layouts: 3.99 us -> 1.75 us
    pallas_call x1, Pallas kernels: 34.8 us -> 25.5 us  [local(): pl.pallas_call(kernel, out_shape=(pltpu.VMEM(back_temp.shape, F32), pltpu...]
    unnamed x2, local copies, waits for them, and re-layouts: 3.99 us -> 1.75 us
where the time goes in v3:
time: 28.1 us; the launch traced here: 27.9 us
  Pallas kernels  25.5 us (91%)
  local copies, waits for them, and re-layouts  1.75 us (6%)
  between operations  0.64 us (2%)
    pallas_call x1, Pallas kernels, local(): pl.pallas_call(kernel, out_shape=(pltpu.VMEM(back_temp.shape, F32), pltpu...  25.5 us
    unnamed x2, local copies, waits for them, and re-layouts  1.75 us

profile of v3, /device:TPU:1, one launch (start us, length us, event | category | flops | bytes accessed | tf_op | source)
XLA Modules:
  0.0 27.9 jit_solution(4302935011791886912)
XLA Ops:
  0.6 25.5 %shard_map.140 = (f32[32,128]{1,0:T(8,128)S(1)}, f32[3,32,32,128]{3,2,1,0:T(8,128)S(1)}) custom-call(f32[32,128]{1,0:T(8,128)} %recovery_temp.1, f32[32,128]{1,0:T(8,128)} %film_coeff.1, f32[32,128]{1,0:T(8,128)} %emissivity.1, f32[32,128]{1,0:T(8,128)} %char_density.1, f32[32,128]{1,0:T(8,128)} %back_temp.1, f32[32,128]{1,0:T(8,128)} %stencil_frac.1, ...), custom_call_target="tpu_custom_call" | custom-call | tf_op jit(solution)/shard_map/pallas_call | solution.py:684
  26.2 0.6 %copy.17 = f32[32,128]{1,0:T(8,128)} copy(f32[32,128]{1,0:T(8,128)S(1)} %get-tuple-element.2) | data formatting | bytes 32768
  26.8 1.1 %copy.18 = f32[3,32,32,128]{3,2,1,0:T(8,128)} copy(f32[3,32,32,128]{3,2,1,0:T(8,128)S(1)} %get-tuple-element.3) | data formatting | bytes 3145728

commit v4 on v3

--- a/solution.py
+++ b/solution.py
@@ -391,6 +391,9 @@
         span(lambda X: relax(read, write, X), 5 + sweep, 35 - sweep, MANY[sweep])
 
     interior(0)
+
+    interior(1)
+    interior(2)
 
     for message in z_far + edges:
         message.wait_recv()
@@ -481,7 +484,7 @@
     for k, step in enumerate(((1, 1, 0), (1, -1, 0), (-1, 1, 0), (-1, -1, 0))):
         clear(back(step), ghost_corner.at[k])
 
-    for sweep in (1, 2, 3):
+    for sweep in (3,):
         interior(sweep)
 
 

time: 28.1 us -> 26.2 us (0.932)
  Pallas kernels: 25.5 us -> 23.6 us
    pallas_call x1, Pallas kernels: 25.5 us -> 23.6 us  [local(): pl.pallas_call(kernel, out_shape=(pltpu.VMEM(back_temp.shape, F32), pltpu...]
where the time goes in v4:
time: 26.2 us; the launch traced here: 26 us
  Pallas kernels  23.6 us (90%)
  local copies, waits for them, and re-layouts  1.75 us (7%)
  between operations  0.64 us (2%)
    pallas_call x1, Pallas kernels, local(): pl.pallas_call(kernel, out_shape=(pltpu.VMEM(back_temp.shape, F32), pltpu...  23.6 us
    unnamed x2, local copies, waits for them, and re-layouts  1.75 us

profile of v4, /device:TPU:1, one launch (start us, length us, event | category | flops | bytes accessed | tf_op | source)
XLA Modules:
  0.0 26.0 jit_solution(6301618005572231908)
XLA Ops:
  0.6 23.6 %shard_map.140 = (f32[32,128]{1,0:T(8,128)S(1)}, f32[3,32,32,128]{3,2,1,0:T(8,128)S(1)}) custom-call(f32[32,128]{1,0:T(8,128)} %recovery_temp.1, f32[32,128]{1,0:T(8,128)} %film_coeff.1, f32[32,128]{1,0:T(8,128)} %emissivity.1, f32[32,128]{1,0:T(8,128)} %char_density.1, f32[32,128]{1,0:T(8,128)} %back_temp.1, f32[32,128]{1,0:T(8,128)} %stencil_frac.1, ...), custom_call_target="tpu_custom_call" | custom-call | tf_op jit(solution)/shard_map/pallas_call | solution.py:687
  24.3 0.6 %copy.17 = f32[32,128]{1,0:T(8,128)} copy(f32[32,128]{1,0:T(8,128)S(1)} %get-tuple-element.2) | data formatting | bytes 32768
  24.9 1.1 %copy.18 = f32[3,32,32,128]{3,2,1,0:T(8,128)} copy(f32[3,32,32,128]{3,2,1,0:T(8,128)S(1)} %get-tuple-element.3) | data formatting | bytes 3145728
